TPU v7x, 32 devices: a whole 2x2x4 slice. The times are simulated.
32 devices in a mesh: rows: 8 (over z, x), tp: 4 (over y, core).
Axes of the slice: x: 2, y: 2, z: 4, core: 2. Of those that a mesh axis runs over, the one named last changes fastest.
Arguments:
- layer_input: bfloat16 [128, 256, 512], P('rows', 'tp'), may hold values from -6 to 6
- segment_labels: int32 [128, 256], P('rows'), may hold values from 0 to 31, never falling along the last dimension, each value on 1 to 24 neighbouring positions
- attend_weight: bfloat16 [3, 512, 512], P(None, None, 'tp'), may hold values from -0.25 to 0.25
- attend_bias: float32 [2, 512], P(None, 'tp'), may hold values from -3 to 3
- out_weight: bfloat16 [512, 512], P('tp'), may hold values from -0.75 to 0.75
- out_bias: float32 [512], replicated, may hold values from -2 to 2
- gain_attention: float32 [512], replicated, may hold values from 0.5 to 1.5
- shift_attention: float32 [512], replicated, may hold values from -2 to 2
- gain_feed: float32 [512], replicated, may hold values from 0.5 to 1.5
- shift_feed: float32 [512], replicated, may hold values from -2 to 2
- up_weight: bfloat16 [512, 2048], P(None, 'tp'), may hold values from -0.25 to 0.25
- up_bias: float32 [2048], P('tp'), may hold values from -3 to 3
- down_weight: bfloat16 [2048, 512], P('tp'), may hold values from -0.1875 to 0.1875
- down_bias: float32 [512], replicated, may hold values from -2 to 2
- pool_weight: bfloat16 [512, 2048], P(None, 'tp'), may hold values from -0.25 to 0.25
- pool_bias: float32 [2048], P('tp'), may hold values from -3 to 3
- hidden_grad: bfloat16 [128, 256, 512], P('rows', 'tp'), may hold values from -6 to 6
- embedding_grad: bfloat16 [128, 32, 2048], P('rows', None, 'tp'), may hold values from -6 to 6
Outputs:
- hidden: bfloat16 [128, 256, 512], P('rows', 'tp')
- embedding: bfloat16 [128, 32, 2048], P('rows', None, 'tp')
- input_grad: bfloat16 [128, 256, 512], P('rows', 'tp')
- attend_weight_grad: float32 [3, 512, 512], P(None, None, 'tp')
- attend_bias_grad: float32 [2, 512], P(None, 'tp')
- out_weight_grad: float32 [512, 512], P('tp')
- out_bias_grad: float32 [512], replicated
- gain_attention_grad: float32 [512], replicated
- shift_attention_grad: float32 [512], replicated
- gain_feed_grad: float32 [512], replicated
- shift_feed_grad: float32 [512], replicated
- up_weight_grad: float32 [512, 2048], P(None, 'tp')
- up_bias_grad: float32 [2048], P('tp')
- down_weight_grad: float32 [2048, 512], P('tp')
- down_bias_grad: float32 [512], replicated
- pool_weight_grad: float32 [512, 2048], P(None, 'tp')
- pool_bias_grad: float32 [2048], P('tp')
Inputs may be any that keep to these rules, and one draw needn't show every extreme that they name: `segment_labels`: in each row labels never fall, start at 0, end at 31, and each label covers 1 to 24 consecutive slots; some segment covers exactly 24.
All inputs are finite; a program needn't handle non-finite values.
Results may differ from a plain program's by a relative error of at most 0.02.
Values may be sent and summed in bfloat16 or wider, within the bound.
A program may use at most 128 MiB of HBM per device.

v0:
```python
import jax
import jax.numpy as jnp
from jax import lax
from jax.sharding import PartitionSpec as P

HEAD_DIM = 64


epsilon = 1e-05
highest = lax.Precision.HIGHEST


def layer_norm(values, gain, shift):
    centred = values - jnp.mean(values, axis=-1, keepdims=True)
    spread_sq = jnp.mean(centred * centred, axis=-1, keepdims=True)
    return centred * lax.rsqrt(spread_sq + epsilon) * gain + shift


def gelu_tanh(values):
    return jax.nn.gelu(values, approximate=True)


def head_scores(query_block, key_block, label_block):
    raw_scores = jnp.einsum(
        "bqhd,bkhd->bhqk", query_block, key_block, preferred_element_type=jnp.float32
    ) * query_block.shape[-1] ** (-0.5)
    allowed = label_block[:, None, :, None] == label_block[:, None, None, :]
    return jnp.where(allowed, raw_scores, -1e30)


def attend_block(inputs):
    query_block, key_block, value_block, label_block = inputs
    masked = head_scores(query_block, key_block, label_block)
    maximum = jnp.max(masked, axis=-1, keepdims=True)
    weights = jnp.exp(masked - maximum)
    totals = jnp.sum(weights, axis=-1, keepdims=True)
    low_weights = (weights / totals).astype(jnp.bfloat16)
    result = jnp.einsum(
        "bhqk,bkhd->bqhd", low_weights, value_block, preferred_element_type=jnp.float32
    )
    return (result.astype(jnp.bfloat16), maximum + jnp.log(totals))


def attend_back(inputs):
    query_block, key_block, value_block, label_block, log_total, grad_block = inputs
    masked = head_scores(query_block, key_block, label_block)
    weights = jnp.exp(masked - log_total)
    grad_weights = jnp.einsum(
        "bqhd,bkhd->bhqk", grad_block, value_block, preferred_element_type=jnp.float32
    )
    grad_values = jnp.einsum(
        "bhqk,bqhd->bkhd",
        weights.astype(jnp.bfloat16),
        grad_block,
        preferred_element_type=jnp.float32,
    )
    centre = jnp.sum(weights * grad_weights, axis=-1, keepdims=True)
    grad_scores = (weights * (grad_weights - centre)).astype(jnp.bfloat16)
    factor = query_block.shape[-1] ** (-0.5)
    grad_queries = (
        jnp.einsum("bhqk,bkhd->bqhd", grad_scores, key_block, preferred_element_type=jnp.float32)
        * factor
    )
    grad_keys = (
        jnp.einsum("bhqk,bqhd->bkhd", grad_scores, query_block, preferred_element_type=jnp.float32)
        * factor
    )
    return (
        grad_queries.astype(jnp.bfloat16),
        grad_keys.astype(jnp.bfloat16),
        grad_values.astype(jnp.bfloat16),
    )


def per_device(
    layer_input,
    segment_labels,
    attend_weight,
    attend_bias,
    out_weight,
    out_bias,
    gain_attention,
    shift_attention,
    gain_feed,
    shift_feed,
    up_weight,
    up_bias,
    down_weight,
    down_bias,
    pool_weight,
    pool_bias,
    hidden_grad,
    embedding_grad,
):
    offset = lax.axis_index("tp") * layer_input.shape[1]
    rows_here, local_slots = (layer_input.shape[0], layer_input.shape[1])
    all_slots = segment_labels.shape[1]
    heads_here = attend_weight.shape[2] // HEAD_DIM
    segment_count = embedding_grad.shape[1]
    earlier = jnp.concatenate([segment_labels[:, :1] - 1, segment_labels[:, :-1]], axis=1)
    local_labels = lax.dynamic_slice_in_dim(segment_labels, offset, local_slots, 1)
    local_first = lax.dynamic_slice_in_dim(segment_labels != earlier, offset, local_slots, 1)
    segment_range = jnp.arange(segment_count, dtype=jnp.int32)
    select_first = (
        (local_labels[:, None, :] == segment_range[None, :, None]) & local_first[:, None, :]
    ).astype(jnp.float32)
    bias_three = jnp.stack([attend_bias[0], jnp.zeros_like(attend_bias[0]), attend_bias[1]])
    pair_rows = 2
    paired_labels = segment_labels.reshape(rows_here // pair_rows, pair_rows, all_slots)

    def split_heads(tensor):
        return tensor.reshape(rows_here // pair_rows, pair_rows, all_slots, heads_here, HEAD_DIM)

    residual_in = layer_input.astype(jnp.float32)
    normed = layer_norm(residual_in, gain_attention, shift_attention).astype(jnp.bfloat16)
    norm_full = lax.all_gather(normed, "tp", axis=1, tiled=True)
    projected = jnp.einsum(
        "rsd,cde->crse", norm_full, attend_weight, preferred_element_type=jnp.float32
    )
    projections = (projected + bias_three[:, None, None, :]).astype(jnp.bfloat16)
    attended, log_total = lax.map(
        attend_block,
        (
            split_heads(projections[0]),
            split_heads(projections[1]),
            split_heads(projections[2]),
            paired_labels,
        ),
    )
    norm_a_full, projections, attended, log_total = (
        norm_full,
        projections,
        attended.reshape(rows_here, all_slots, heads_here * HEAD_DIM),
        log_total,
    )
    attention_terms = jnp.einsum(
        "rse,ed->rsd", attended, out_weight, preferred_element_type=jnp.float32
    )
    middle = (
        residual_in
        + lax.psum_scatter(
            attention_terms.astype(jnp.bfloat16), "tp", scatter_dimension=1, tiled=True
        ).astype(jnp.float32)
        + out_bias
    )
    normed = layer_norm(middle, gain_feed, shift_feed).astype(jnp.bfloat16)
    norm_full = lax.all_gather(normed, "tp", axis=1, tiled=True)
    preact = (
        jnp.einsum("rsd,df->rsf", norm_full, up_weight, preferred_element_type=jnp.float32)
        + up_bias
    )
    norm_f_full, preact = (norm_full, preact)
    activated = gelu_tanh(preact).astype(jnp.bfloat16)
    feed_terms = jnp.einsum(
        "rsf,fd->rsd", activated, down_weight, preferred_element_type=jnp.float32
    )
    residual_out = (
        middle
        + lax.psum_scatter(
            feed_terms.astype(jnp.bfloat16), "tp", scatter_dimension=1, tiled=True
        ).astype(jnp.float32)
        + down_bias
    )
    pooled_terms = jnp.einsum("rcs,rsd->rcd", select_first, residual_out, precision=highest)
    pooled = lax.psum(pooled_terms.astype(jnp.bfloat16), "tp")
    embedding = (
        jnp.einsum("rcd,do->rco", pooled, pool_weight, preferred_element_type=jnp.float32)
        + pool_bias
    ).astype(jnp.bfloat16)
    pool_weight_grad = jnp.einsum(
        "rcd,rco->do", pooled, embedding_grad, preferred_element_type=jnp.float32
    )
    pool_bias_grad = jnp.sum(embedding_grad.astype(jnp.float32), axis=(0, 1))
    pool_terms = jnp.einsum(
        "rco,do->rcd", embedding_grad, pool_weight, preferred_element_type=jnp.float32
    )
    grad_pool = lax.psum(pool_terms.astype(jnp.bfloat16), "tp").astype(jnp.float32)
    grad_resid = hidden_grad.astype(jnp.float32) + jnp.einsum(
        "rcs,rcd->rsd", select_first, grad_pool, precision=highest
    )
    grad_branch_f = grad_resid.astype(jnp.bfloat16)
    down_bias_grad = jnp.sum(grad_branch_f.astype(jnp.float32), axis=(0, 1))
    grad_f_full = lax.all_gather(grad_branch_f, "tp", axis=1, tiled=True)
    down_weight_grad = jnp.einsum(
        "rsf,rsd->fd", activated, grad_f_full, preferred_element_type=jnp.float32
    )
    grad_activated = jnp.einsum(
        "rsd,fd->rsf", grad_f_full, down_weight, preferred_element_type=jnp.float32
    )
    grad_preact = jax.vjp(gelu_tanh, preact)[1](grad_activated)[0].astype(jnp.bfloat16)
    up_weight_grad = jnp.einsum(
        "rsd,rsf->df", norm_f_full, grad_preact, preferred_element_type=jnp.float32
    )
    up_bias_grad = jnp.sum(grad_preact.astype(jnp.float32), axis=(0, 1))
    feed_back_terms = jnp.einsum(
        "rsf,df->rsd", grad_preact, up_weight, preferred_element_type=jnp.float32
    )
    grad_norm_f = lax.psum_scatter(
        feed_back_terms.astype(jnp.bfloat16), "tp", scatter_dimension=1, tiled=True
    ).astype(jnp.float32)
    feed_pull = jax.vjp(layer_norm, middle, gain_feed, shift_feed)[1]
    grad_from_norm, gain_feed_grad, shift_feed_grad = feed_pull(grad_norm_f)
    grad_middle = grad_resid + grad_from_norm
    grad_branch_a = grad_middle.astype(jnp.bfloat16)
    out_bias_grad = jnp.sum(grad_branch_a.astype(jnp.float32), axis=(0, 1))
    grad_a_full = lax.all_gather(grad_branch_a, "tp", axis=1, tiled=True)
    out_weight_grad = jnp.einsum(
        "rse,rsd->ed", attended, grad_a_full, preferred_element_type=jnp.float32
    )
    grad_attended = jnp.einsum(
        "rsd,ed->rse", grad_a_full, out_weight, preferred_element_type=jnp.float32
    ).astype(jnp.bfloat16)
    grad_queries, grad_keys, grad_values = lax.map(
        attend_back,
        (
            split_heads(projections[0]),
            split_heads(projections[1]),
            split_heads(projections[2]),
            paired_labels,
            log_total,
            split_heads(grad_attended),
        ),
    )
    grad_project = jnp.stack([grad_queries, grad_keys, grad_values]).reshape(
        3, rows_here, all_slots, heads_here * HEAD_DIM
    )
    attend_weight_grad = jnp.einsum(
        "rsd,crse->cde", norm_a_full, grad_project, preferred_element_type=jnp.float32
    )
    grad_sums = jnp.sum(grad_project.astype(jnp.float32), axis=(1, 2))
    attend_bias_grad = jnp.stack([grad_sums[0], grad_sums[2]])
    attend_back_terms = jnp.einsum(
        "crse,cde->rsd", grad_project, attend_weight, preferred_element_type=jnp.float32
    )
    grad_norm_a = lax.psum_scatter(
        attend_back_terms.astype(jnp.bfloat16), "tp", scatter_dimension=1, tiled=True
    ).astype(jnp.float32)
    input_pull = jax.vjp(layer_norm, residual_in, gain_attention, shift_attention)[1]
    grad_input_norm, gain_attention_grad, shift_attention_grad = input_pull(grad_norm_a)
    input_grad = (grad_middle + grad_input_norm).astype(jnp.bfloat16)
    (
        out_bias_grad,
        gain_attention_grad,
        shift_attention_grad,
        gain_feed_grad,
        shift_feed_grad,
        down_bias_grad,
    ) = lax.psum(
        (
            out_bias_grad,
            gain_attention_grad,
            shift_attention_grad,
            gain_feed_grad,
            shift_feed_grad,
            down_bias_grad,
        ),
        ("rows", "tp"),
    )
    hidden_out = residual_out.astype(jnp.bfloat16)
    (
        attend_weight_grad,
        attend_bias_grad,
        out_weight_grad,
        up_weight_grad,
        up_bias_grad,
        down_weight_grad,
        pool_weight_grad,
        pool_bias_grad,
    ) = lax.psum(
        (
            attend_weight_grad,
            attend_bias_grad,
            out_weight_grad,
            up_weight_grad,
            up_bias_grad,
            down_weight_grad,
            pool_weight_grad,
            pool_bias_grad,
        ),
        "rows",
    )
    return (
        hidden_out,
        embedding,
        input_grad,
        attend_weight_grad,
        attend_bias_grad,
        out_weight_grad,
        out_bias_grad,
        gain_attention_grad,
        shift_attention_grad,
        gain_feed_grad,
        shift_feed_grad,
        up_weight_grad,
        up_bias_grad,
        down_weight_grad,
        down_bias_grad,
        pool_weight_grad,
        pool_bias_grad,
    )


def solution(mesh):
    placed = (
        P("rows", "tp", None),
        P("rows", None),
        P(None, None, "tp"),
        P(None, "tp"),
        P("tp", None),
        P(),
        P(),
        P(),
        P(),
        P(),
        P(None, "tp"),
        P("tp"),
        P("tp", None),
        P(),
        P(None, "tp"),
        P("tp"),
        P("rows", "tp", None),
        P("rows", None, "tp"),
    )
    return jax.shard_map(
        per_device,
        mesh=mesh,
        in_specs=placed,
        out_specs=(
            P("rows", "tp", None),
            P("rows", None, "tp"),
            P("rows", "tp", None),
            P(None, None, "tp"),
            P(None, "tp"),
            P("tp", None),
            P(),
            P(),
            P(),
            P(),
            P(),
            P(None, "tp"),
            P("tp"),
            P("tp", None),
            P(),
            P(None, "tp"),
            P("tp"),
        ),
        check_vma=False,
    )
```

profile of v0, /device:TPU:0, one launch (start us, length us, event | category | flops | bytes accessed | tf_op | source)
XLA Modules:
  0.0 766.5 jit_solution(15101855873631255972)
XLA Ops:
  12.4 37.1 %all-gather.5.cloned.1.call-done = bf16[16,256,512]{2,1,0:T(8,128)(2,1)} async-done(((bf16[16,64,512]{2,1,0:T(8,128)(2,1)}), bf16[16,256,512]{2,1,0:T(8,128)(2,1)}) %all-gather.5.cloned.1.call-update) | async-done | bytes 4194320 | tf_op jit(solution)/shard_map/all_gather | solution.py:116
  49.5 4.0 fusion.58
  56.4 28.5 %while.26 = (s32[]{:T(128)}, bf16[8,2,256,2,64]{2,4,3,1,0:T(8,128)(2,1)}, f32[8,2,2,256,1]{3,2,1,4,0:T(2,128)S(1)}, bf16[8,2,256,2,64]{2,4,3,1,0:T(8,128)(2,1)},...) while((s32[]{:T(128)}, ...), condition=%wide.region_5.6_spmd, body=%wide.region_2.5_spmd.sunk | while | flops 69401600 | bytes 3973221 | solution.py:121
  58.0 1.9 fusion.153
  61.6 1.9 fusion.153
  65.2 1.9 fusion.153
  68.7 1.9 fusion.153
  72.3 1.9 fusion.153
  75.9 1.9 fusion.153
  79.5 1.9 fusion.153
  83.0 1.9 fusion.153
  84.9 4.4 convolution_convert_fusion.4
  89.5 44.6 %reduce-scatter.5.cloned.1.call-done = bf16[16,64,512]{2,1,0:T(8,128)(2,1)} async-done(((bf16[16,256,512]{2,1,0:T(8,128)(2,1)}), bf16[16,64,512]{2,1,0:T(8,128)(2,1)}) %reduce-scatter.5.cloned.1.call-update) | async-done | bytes 1048592 | tf_op jit(solution)/shard_map/reduce_scatter | solution.py:141
  138.1 34.6 %all-gather.7.cloned.1.call-done = bf16[16,256,512]{2,1,0:T(8,128)(2,1)} async-done(((bf16[16,64,512]{2,1,0:T(8,128)(2,1)}), bf16[16,256,512]{2,1,0:T(8,128)(2,1)}) %all-gather.7.cloned.1.call-update) | async-done | bytes 4194320 | tf_op jit(solution)/shard_map/all_gather | solution.py:147
  172.7 4.6 fusion.93
  177.4 3.2 copy-done.5
  180.6 5.0 convolution_convert_fusion.3
  186.6 2.3 convolution_convert_fusion.6
  188.9 41.4 %reduce-scatter.7.cloned.1.call-done = bf16[16,64,512]{2,1,0:T(8,128)(2,1)} async-done(((bf16[16,256,512]{2,1,0:T(8,128)(2,1)}), bf16[16,64,512]{2,1,0:T(8,128)(2,1)}) %reduce-scatter.7.cloned.1.call-update) | async-done | bytes 1048592 | tf_op jit(solution)/shard_map/reduce_scatter | solution.py:159
  230.3 3.4 convolution_convert_fusion.7
  233.7 36.3 %all-reduce.9.cloned.1.call-done = (bf16[16,32,512]{2,1,0:T(8,128)(2,1)}, bf16[16,32,512]{2,1,0:T(8,128)(2,1)}) async-done(((bf16[16,32,512]{2,1,0:T(8,128)(2,1)}, bf16[16,32,512]{2,1,0:T(8,128)(2,1)}), (bf16[16,32,512]{2,1,0:T(8,128)(2,1)}, bf16[16,32,512]{2,1,0:T(8,128)(2,1)})) %all-reduce.9.cloned.1.call-update) | async-done | bytes 1048592 | tf_op jit(solution)/shard_map/psum | solution.py:165
  270.0 3.6 convert_reduce_fusion.5
  273.6 35.0 %all-gather.9.cloned.1.call-done = bf16[16,256,512]{2,1,0:T(8,128)(2,1)} async-done(((bf16[16,64,512]{2,1,0:T(8,128)(2,1)}), bf16[16,256,512]{2,1,0:T(8,128)(2,1)}) %all-gather.9.cloned.1.call-update) | async-done | bytes 4194320 | tf_op jit(solution)/shard_map/all_gather | solution.py:183
  308.6 10.4 %convert_reduce_fusion = (f32[512]{0:T(512)S(1)}, bf16[16,256,512]{2,1,0:T(8,128)(2,1)S(1)}) fusion(f32[16,256,512]{2,1,0:T(8,128)} %copy-done.5, f32[512]{0:T(512)S(1)} %copy-done.36, bf16[16,256,512]{2,1,0:T(8,128)(2,1)} %all-gather.9.cloned.1.call-done, bf16[512,512]{1,0:T(8,128)(2,1)S(1)} %copy-done), kind=kOutput, calls=%fused_computation.73 | convolution fusion | flops 2195717632 | bytes 17305600 | tf_op jit(solution)/shard_map/rsd,fd->rsf/dot_general | solution.py:187
  319.0 2.0 copy-done.8
  321.0 4.3 convolution_convert_fusion.2
  325.4 44.6 %reduce-scatter.9.cloned.1.call-done = bf16[16,64,512]{2,1,0:T(8,128)(2,1)} async-done(((bf16[16,256,512]{2,1,0:T(8,128)(2,1)}), bf16[16,64,512]{2,1,0:T(8,128)(2,1)}) %reduce-scatter.9.cloned.1.call-update) | async-done | bytes 1048592 | tf_op jit(solution)/shard_map/reduce_scatter | solution.py:198
  370.0 2.5 convert_reduce_fusion.3
  374.1 1.9 convert_reduce_fusion.6
  378.9 5.8 convolution_bitcast_fusion.2
  384.8 4.8 convolution_bitcast_fusion.1
  389.5 21.2 %all-gather.11.cloned.1.call-done = bf16[16,256,512]{2,1,0:T(8,128)(2,1)} async-done(((bf16[16,64,512]{2,1,0:T(8,128)(2,1)}), bf16[16,256,512]{2,1,0:T(8,128)(2,1)}) %all-gather.11.cloned.1.call-update) | async-done | bytes 4194320 | tf_op jit(solution)/shard_map/all_gather | solution.py:206
  410.7 4.6 convolution_convert_fusion.5
  418.6 68.7 %while.27 = (s32[]{:T(128)}, bf16[8,2,256,2,64]{2,4,3,1,0:T(8,128)(2,1)}, bf16[8,2,256,2,64]{2,4,3,1,0:T(8,128)(2,1)}, bf16[8,2,256,2,64]{2,4,3,1,0:T(8,128)(2,1...) while((s32[]{:T(128)}, ...), condition=%wide.region_17.18_spmd, body=%wide.region_15.17_spmd.sunk | while | flops 170589184 | bytes 9469053 | solution.py:213
  421.7 1.9 fusion.166
  423.6 1.8 fusion.165
  430.3 1.9 fusion.166
  432.2 1.8 fusion.165
  438.9 1.9 fusion.166
  440.8 1.8 fusion.165
  447.5 1.9 fusion.166
  449.4 1.8 fusion.165
  456.1 1.9 fusion.166
  458.0 1.8 fusion.165
  464.7 1.9 fusion.166
  466.5 1.8 fusion.165
  473.3 1.9 fusion.166
  475.1 1.8 fusion.165
  481.9 1.9 fusion.166
  483.7 1.8 fusion.165
  487.3 2.3 copy.55
  489.6 2.3 copy.53
  491.9 2.3 copy.54
  494.1 4.1 convolution_bitcast_fusion.3
  498.2 4.9 fusion.80
  504.1 6.3 bitcast_convert_fusion
  511.5 2.3 fusion.83
  515.5 24.1 %all-reduce.1 = (f32[2,128]{1,0:T(2,128)}, f32[512]{0:T(512)}, f32[512]{0:T(512)}) all-reduce(f32[2,128]{1,0:T(2,128)S(1)} %pad_maximum_fusion.2, f32[512]{0:T(512)S(1)} %get-tuple-element.224, f32[512]{0:T(512)S(1)} %convert_reduce_fusion.7), channel_id=1, replica_groups=mesh['rows'=8,'tp'=4] {'rows'}, use_global_device_ids=true, to_apply=%region_23.24 | all-reduce | flops 1280 | bytes 10240 | tf_op jit(solution)/shard_map/psum | solution.py:269
  539.6 122.2 %all-reduce.7.cloned.1.call-done = (f32[3,512,128]{1,2,0:T(8,128)}, f32[128,512]{1,0:T(8,128)}, f32[512,512]{1,0:T(8,128)}, f32[512,512]{1,0:T(8,128)}, f32[512,512]{1,0:T(8,128)}) async-done(((f32[3,512,128]{1,2,0:T(8,128)}, f32[128,512]{1,0:T(8,128)}, f32[512,512]{1,0:T(8,128)}, f32[512,512]{1,0:T(8,128)}, f32[512,512]{1,0:T(8,128)}), (f32[3,512,128]{1,2,0:T(8,128)}, f32[128,512]{1,0:T(8,128)}, ...) | async-done | bytes 4194320 | tf_op jit(solution)/shard_map/psum | solution.py:269
  661.8 2.3 copy.58
  664.1 43.4 %reduce-scatter.11.cloned.1.call-done = bf16[16,64,512]{2,1,0:T(8,128)(2,1)} async-done(((bf16[16,256,512]{2,1,0:T(8,128)(2,1)}), bf16[16,64,512]{2,1,0:T(8,128)(2,1)}) %reduce-scatter.11.cloned.1.call-update) | async-done | bytes 1048592 | tf_op jit(solution)/shard_map/reduce_scatter | solution.py:235
  707.5 2.4 convert_reduce_fusion.2
  711.3 39.6 %all-reduce = (f32[512]{0:T(512)}, f32[512]{0:T(512)}, f32[512]{0:T(512)}, f32[512]{0:T(512)}, f32[512]{0:T(512)}, /*index=5*/f32[512]{0:T(512)}) all-reduce(f32[512]{0:T(512)S(1)} %get-tuple-element.208, f32[512]{0:T(512)S(1)} %get-tuple-element.150, ...), channel_id=1, replica_groups=mesh['rows'=8,'tp'=4] {'rows','tp'}, use_global_device_ids=true, to_apply=%region_26.27 | all-reduce | flops 3072 | bytes 24576 | tf_op jit(solution)/shard_map/psum | solution.py:248
  750.8 4.8 add_convert_fusion.1
  (233 shorter events, 81.8 us)
Async XLA Ops:
  7.2 173.4 %copy-start = (bf16[512,512]{1,0:T(8,128)(2,1)S(1)}, bf16[512,512]{1,0:T(8,128)(2,1)}, u32[]{:S(2)}) copy-start(bf16[512,512]{1,0:T(8,128)(2,1)} %param.34) | copy-start | bytes 1572868
  7.2 3.5 copy-start.2
  7.2 3.4 copy-start.27
  7.2 3.4 copy-start.28
  7.2 42.2 %all-gather.5.cloned.1.call-start = ((), (), s32[]{:S(2)}) async-start(), calls=%async_computation.4 | async-start | bytes 5242880 | tf_op jit(solution)/shard_map/all_gather | solution.py:116
  8.8 3.4 copy-start.24
  8.9 3.4 copy-start.31
  8.9 40.6 %copy-start.34 = (bf16[3,512,128]{2,1,0:T(8,128)(2,1)S(1)}, bf16[3,512,128]{2,1,0:T(8,128)(2,1)}, u32[]{:S(2)}) copy-start(bf16[3,512,128]{2,1,0:T(8,128)(2,1)} %param.24) | copy-start | bytes 1179652
  12.1 122.0 %reduce-scatter.5.cloned.1.call-start = ((), (), s32[]{:S(2)}) async-start(), calls=%async_computation.5 | async-start | bytes 5242880 | tf_op jit(solution)/shard_map/reduce_scatter | solution.py:141
  56.4 28.6 %copy-start.22 = (bf16[128,512]{1,0:T(8,128)(2,1)S(1)}, bf16[128,512]{1,0:T(8,128)(2,1)}, u32[]{:S(2)}) copy-start(bf16[128,512]{1,0:T(8,128)(2,1)} %param.26) | copy-start | bytes 393220
  89.4 44.7 %copy-start.25 = (f32[512]{0:T(512)S(1)}, f32[512]{0:T(512)}, u32[]{:S(2)}) copy-start(f32[512]{0:T(512)} %param.27) | copy-start | bytes 6148
  89.4 47.0 %copy-start.26 = (f32[512]{0:T(512)S(1)}, f32[512]{0:T(512)}, u32[]{:S(2)}) copy-start(f32[512]{0:T(512)} %param.30) | copy-start | bytes 6148
  89.4 47.0 %copy-start.29 = (f32[512]{0:T(512)S(1)}, f32[512]{0:T(512)}, u32[]{:S(2)}) copy-start(f32[512]{0:T(512)} %param.31) | copy-start | bytes 6148
  89.4 83.3 %all-gather.7.cloned.1.call-start = ((), (), s32[]{:S(2)}) async-start(), calls=%async_computation.6 | async-start | bytes 5242880 | tf_op jit(solution)/shard_map/all_gather | solution.py:147
  134.1 1.7 copy-start.3
  136.5 36.3 %copy-start.19 = (bf16[512,512]{1,0:T(8,128)(2,1)S(1)}, bf16[512,512]{1,0:T(8,128)(2,1)}, u32[]{:S(2)}) copy-start(bf16[512,512]{1,0:T(8,128)(2,1)} %param.32) | copy-start | bytes 1572868
  138.1 42.5 %copy-start.36 = (f32[512]{0:T(512)S(1)}, f32[512]{0:T(512)}, u32[]{:S(2)}) copy-start(f32[512]{0:T(512)} %param.33) | copy-start | bytes 6148
  138.1 92.2 %reduce-scatter.7.cloned.1.call-start = ((), (), s32[]{:S(2)}) async-start(), calls=%async_computation.7 | async-start | bytes 5242880 | tf_op jit(solution)/shard_map/reduce_scatter | solution.py:159
  177.3 3.2 copy-start.5
  185.5 1.0 copy-start.15
  185.5 44.7 %copy-start.30 = (f32[512]{0:T(512)S(1)}, f32[512]{0:T(512)}, u32[]{:S(2)}) copy-start(f32[512]{0:T(512)} %param.35) | copy-start | bytes 6148
  185.6 84.4 %all-reduce.9.cloned.1.call-start = ((), (), s32[]{:S(2)}) async-start(), calls=%async_computation.13 | async-start | bytes 2097152 | tf_op jit(solution)/shard_map/psum | solution.py:165
  233.6 75.0 %all-gather.9.cloned.1.call-start = ((), (), s32[]{:S(2)}) async-start(), calls=%async_computation.8 | async-start | bytes 5242880 | tf_op jit(solution)/shard_map/all_gather | solution.py:183
  273.6 96.4 %reduce-scatter.9.cloned.1.call-start = ((), (), s32[]{:S(2)}) async-start(), calls=%async_computation.9 | async-start | bytes 5242880 | tf_op jit(solution)/shard_map/reduce_scatter | solution.py:198
  308.6 12.4 %copy-start.20 = (bf16[512,512]{1,0:T(8,128)(2,1)S(1)}, bf16[512,512]{1,0:T(8,128)(2,1)}, u32[]{:S(2)}) copy-start(bf16[512,512]{1,0:T(8,128)(2,1)} %param.32) | copy-start | bytes 1572868
  319.0 2.0 copy-start.8
  325.3 85.4 %all-gather.11.cloned.1.call-start = ((), (), s32[]{:S(2)}) async-start(), calls=%async_computation.10 | async-start | bytes 5242880 | tf_op jit(solution)/shard_map/all_gather | solution.py:206
  370.0 2.5 copy-start.7
  372.5 1.6 copy-start.6
  374.1 2.2 copy-start.33
  376.1 285.7 %all-reduce.7.cloned.1.call-start = ((), (), s32[]{:S(2)}) async-start(), calls=%async_computation.12 | async-start | bytes 8388608 | tf_op jit(solution)/shard_map/psum | solution.py:269
  376.3 2.6 copy-start.4
  376.3 8.4 %slice-start = ((s8[8388608]{0:T(1024)(128)(4,1)}), s8[4194304]{0:T(1024)(128)(4,1)S(1)}, s32[]{:S(2)}) async-start(s8[8388608]{0:T(1024)(128)(4,1)} %bitcast.190), calls=%async_computation.14 | async-start | bytes 8388608
  378.9 5.9 slice-start.1
  378.9 5.9 copy-start.32
  494.1 4.1 copy-start.10
  494.1 4.1 copy-start.12
  494.1 4.1 copy-start.14
  503.1 1.0 copy-start.35
  503.1 204.4 %reduce-scatter.11.cloned.1.call-start = ((), (), s32[]{:S(2)}) async-start(), calls=%async_computation.11 | async-start | bytes 5242880 | tf_op jit(solution)/shard_map/reduce_scatter | solution.py:235
  510.4 1.0 copy-start.21
  510.4 1.0 copy-start.37
  510.4 3.3 copy-start.11
  510.5 3.3 copy-start.13
  707.5 2.4 copy-start.9
  750.8 4.8 copy-start.23
  750.8 5.5 copy-start.18
  755.6 1.7 copy-start.17
  756.3 1.9 copy-start.16
  756.3 2.9 copy-start.1
Sparse Core Ops, SparseCore 0:
  12.3 37.1 all-gather.4
  89.5 44.5 reduce-scatter.4
  138.2 34.4 all-gather.6
  185.7 44.5 reduce-scatter.6
  233.7 36.1 all-reduce.8
  273.7 34.8 all-gather.8
  325.4 44.5 reduce-scatter.8
  376.2 34.4 all-gather.10
  503.2 158.5 all-reduce.6
  664.2 43.2 reduce-scatter.10
where the time goes:
time: 776 us; the launch traced here: 767 us
  waiting for transfers between devices  460 us (59%)
  matrix products  168 us (22%)
  blocking collectives  63.6 us (8%)
  other arithmetic  30.1 us (4%)
  local copies, waits for them, and re-layouts  27.9 us (4%)
  between operations  15.1 us (2%)
    psum x1, waiting for transfers between devices, per_device(): lax.psum((attend_weight_grad, attend_bias_grad, out_weight_grad, up_weigh...  122 us
    all_gather x2, waiting for transfers between devices, per_device(): norm_full = lax.all_gather(normed, 'tp', axis=1, tiled=True)  71.7 us
    reduce_scatter x1, waiting for transfers between devices, per_device(): lax.psum_scatter(feed_back_terms.astype(jnp.bfloat16), 'tp', scatter_dime...  44.6 us
    reduce_scatter x1, waiting for transfers between devices, per_device(): lax.psum_scatter(attention_terms.astype(jnp.bfloat16), 'tp', scatter_dime...  44.6 us
    reduce_scatter x1, waiting for transfers between devices, per_device(): lax.psum_scatter(attend_back_terms.astype(jnp.bfloat16), 'tp', scatter_di...  43.4 us
    reduce_scatter x1, waiting for transfers between devices, per_device(): lax.psum_scatter(feed_terms.astype(jnp.bfloat16), 'tp', scatter_dimension...  41.4 us
    psum x1, blocking collectives, per_device(): lax.psum((out_bias_grad, gain_attention_grad, shift_attention_grad, gain_...  39.6 us
    psum x1, waiting for transfers between devices, per_device(): pooled = lax.psum(pooled_terms.astype(jnp.bfloat16), 'tp')  36.3 us
  transfers between devices with their start and end apart: 10, of which 10 were waited for; matrix products, arithmetic and copies ran while one was open for 4% of the time, Pallas kernels for 0%

commit v1 on v0

v1 whole, which is shorter than its diff:
```python
import functools
import math

import jax
import jax.numpy as jnp
from jax import lax
from jax.experimental import pallas as pl
from jax.experimental.pallas import tpu as pltpu
from jax.sharding import PartitionSpec as P

MESH = pl.DeviceIdType.MESH
HEAD_DIM = 64
HALO = 32
EPS = 1e-5
BF = jnp.bfloat16
F32 = jnp.float32
ROOT = math.sqrt(2.0 / math.pi)
CUBE = 0.044715
NAMES = ("dna", "dnb", "upa", "upb", "o", "q", "k", "v", "pl")
X_FIRST = ("dna", "upa")
PLAN = (
    (),
    (),
    (),
    (),
    (),
    (),
    (),
    (),
    (),
    (),
    ("qkv.step1", "gpool.step2", "wo.step1"),
    ("up.step1", "qkv.rx", "qkv.rz", "dn.step1", "wo.rx", "qkv.rxz"),
    ("wo.rz",),
    ("wo.rxz",),
    (),
    ("up.rx",),
    (),
    ("up.rz",),
    (),
    (),
    (),
    (),
    ("dn.rx", "up.rxz"),
    ("gpool.step3",),
    (),
    ("dn.rz",),
    (),
    (),
    ("dn.rxz",),
    (),
    (),
    (),
    (),
    (),
    (),
    (),
    (),
    (),
    ("pooled.step2",),
    (),
    (),
    ("dnb.y",),
    ("dna.x",),
    (),
    ("pooled.step3",),
    (),
    (),
    ("pl.x",),
    ("dna.y",),
    ("dnb.x",),
    (),
    ("upb.y",),
    ("upa.x",),
    (),
    (),
    ("dna.z", "o.y"),
    (),
    ("pl.z",),
    (),
    (),
    (),
    ("dnb.z", "upb.x"),
    ("dna.gz", "v.y", "o.x"),
    ("k.y",),
    ("upa.y",),
    ("q.y", "pl.gz"),
    ("upb.z", "v.x"),
    ("dnb.gz", "o.z"),
    ("dna.gx", "upa.z", "v.z", "k.x", "sm.s0", "pl.gx"),
    (),
    ("upb.gz", "q.x"),
    ("dnb.gx", "sm.s1", "k.z"),
    ("dna.end", "o.gz", "late.tp", "upa.gz", "v.gz", "pl.end", "q.z", "upb.gx", "k.gz", "dnb.end", "sm.s2", "o.gx", "late.rows", "upb.end", "upa.gx", "o.end", "v.gx", "q.gz", "k.gx", "upa.end", "v.end", "sm.s3", "k.end", "q.gx", "q.end"),
)


def mm(a, b):
    return jnp.dot(a, b, preferred_element_type=F32)


def mm_t(a, b):
    return lax.dot_general(a, b, (((1,), (1,)), ((), ())), preferred_element_type=F32)


def t_mm(a, b):
    return lax.dot_general(a, b, (((0,), (0,)), ((), ())), preferred_element_type=F32)


def normalize(values):
    mean = jnp.mean(values, axis=-1, keepdims=True)
    centred = values - mean
    spread = jnp.mean(centred * centred, axis=-1, keepdims=True)
    factor = lax.rsqrt(spread + EPS)
    return centred * factor, factor


def norm_back(grad, unit, factor, gain):
    scaled = grad * gain
    first = jnp.mean(scaled, axis=-1, keepdims=True)
    second = jnp.mean(scaled * unit, axis=-1, keepdims=True)
    return factor * (scaled - first - unit * second)


def total(values):
    return jnp.sum(values, axis=0, keepdims=True)


def layer_kernel(dims, *refs):
    (groups, RH, LS, D, FF, SEGS) = dims
    W = LS + 2 * HALO
    (x_in, lab_in, wqkv_in, ab_in, wo_in, v0_in, v1_in, v2_in, v3_in, v4_in, wup_in, bup_in, wdn_in, v5_in, wp_in, bp_in, hg_in, eg_in,
     hid_out, emb_out, ig_out, gdn_out, gup_out, go_out, gq_out, gk_out, gv_out, gpl_out, sm_out, late_out,
     x, hg, eg, mask, codes, wqkv, wo, wup, wdn, wp, shared, vec, bup,
     nw, q, k, v, p, at, mid, nf, act, dact, gma, gat, hid, gnc,
     halo_l, halo_r, halo_fl, halo_fr,
     gpt, gpr1, gpr2, gps, pt, pr1, pr2, ps, emb,
     smalls, sm_r, late, late_tp, late_rows,
     *tail) = refs
    tail = list(tail)
    sets = {}
    for name in NAMES:
        sets[name] = [tail.pop(0) for _ in range(4 if name == "pl" else 6)]
    if groups > 1:
        r5 = {name: tail.pop(0) for name in NAMES + ("sm", "late")}
    send_sems, recv_sems, local_sems = tail
    T = RH * LS
    BR = 4
    NB = RH // BR
    BT = BR * LS
    H2 = 4 * HEAD_DIM

    r, t = lax.axis_index("rows"), lax.axis_index("tp")
    core, ypos = t % 2, t // 2
    tc = t + 1 - 2 * core
    ty = (t + 2) % 4
    tdiag = 3 - t
    xpos = r % 2
    rx = r + 1 - 2 * xpos
    zpos = (r // 2) % 4
    base = (r // 8) * 8
    zpeers = [base + ((zpos + dz) % 4) * 2 + xpos for dz in (1, 2, 3)]
    quad = r % 4
    rz = r + 2 - 4 * (quad // 2)
    rxz = rz + 1 - 2 * xpos
    xzpeers = [base + ((zpos + dz) % 4) * 2 + 1 - xpos for dz in (1, 2, 3)]
    gpeers = [((r // 8 + dg) % groups) * 8 + r % 8 for dg in range(1, groups)]

    counter = [0]

    def remote(src, dst, dev):
        i = counter[0]
        counter[0] += 1
        return pltpu.make_async_remote_copy(
            src_ref=src, dst_ref=dst, send_sem=send_sems.at[i], recv_sem=recv_sems.at[i],
            device_id=dev, device_id_type=MESH)

    local_count = [0]

    def local(src, dst):
        i = local_count[0]
        local_count[0] += 1
        c = pltpu.make_async_copy(src, dst, local_sems.at[i])
        c.start()
        return c

    spot, steps = [0], {}

    def chain(name, *links):
        for label, fn, _ in links:
            steps[name + "." + label] = fn

    def live(*names):
        pass

    def take(i):
        for name in PLAN[i] if i < len(PLAN) else ():
            steps[name]()

    def point():
        spot[0] += 1
        take(spot[0] - 1)

    def must(*names):
        point()

    def run(name, count, body, polls=None):
        first = spot[0]
        spot[0] += count

        def step(b, carry):
            body(b)
            for i in range(count):
                if i in (polls or {}) or (first + i < len(PLAN) and PLAN[first + i]):
                    @pl.when(b == i)
                    def _():
                        if i in (polls or {}):
                            polls[i]()
                        take(first + i)
            return carry

        lax.fori_loop(0, count, step, 0)

    def once(name, fn):
        fn()
        point()

    pending = []

    def go(copy):
        copy.start()
        pending.append(copy)
        return copy

    load_x = local(x_in, x)
    load_wp = local(wp_in, wp)
    load_eg = local(eg_in, eg)
    barrier = pltpu.get_barrier_semaphore()
    friends = [(r, tc), (r, ty), (r, tdiag), (rx, t)] + [(zp, t) for zp in zpeers + xzpeers] + [(gp_, t) for gp_ in gpeers]
    for dev in friends:
        pl.semaphore_signal(barrier, inc=1, device_id=dev, device_id_type=MESH)
    pl.semaphore_wait(barrier, len(friends))

    shared[t, 0:2, :] = ab_in[...]
    shared[t, 2:6, :] = bup_in[...]
    bias_moves = [go(remote(shared.at[t], shared.at[t], (r, dev))) for dev in (tc, ty, tdiag)]
    full = {"qkv": wqkv, "wo": wo, "up": wup, "dn": wdn}
    given = {"qkv": wqkv_in, "wo": wo_in, "up": wup_in, "dn": wdn_in}

    def shard(name, s, piece=None):
        ref = full[name]
        if name in ("qkv", "up"):
            rows_ = pl.ds(0, D) if piece is None else pl.ds(piece * (D // 4), D // 4)
            if name == "qkv":
                return ref.at[:, rows_, pl.ds(pl.multiple_of(s * 128, 128), 128)]
            return ref.at[rows_, pl.ds(pl.multiple_of(s * (FF // 4), 128), FF // 4)]
        n = (D if name == "wo" else FF) // 4
        if piece is None:
            return ref.at[pl.ds(s * n, n)]
        return ref.at[pl.ds(s * n + piece * (n // 4), n // 4)]

    def own_piece(name, piece):
        ref = given[name]
        if name == "qkv":
            return ref.at[:, pl.ds(piece * (D // 4), D // 4)]
        n = ref.shape[0] // 4
        return ref.at[pl.ds(piece * n, n)]

    class Gather:
        def __init__(self, name):
            self.name = name
            self.y = go(remote(own_piece(name, quad), shard(name, t, quad), (r, ty)))
            self.c = go(remote(given[name], shard(name, t), (r, tc)))
            self.loc = local(given[name], shard(name, t))
            mine = shard(name, ty, quad)
            self.x = [remote(mine, mine, (dev, t)) for dev in (rx, rz, rxz)]
            self.f = [remote(mine, mine, (r, tc))]
            for dev in (rx, rz, rxz):
                got = shard(name, ty, dev % 4)
                self.f.append(remote(got, got, (r, tc)))
            chain(name, ("step1", self.step1, [self.y]), ("rx", lambda: self.step2(0), [self.x[0]]),
                  ("rz", lambda: self.step2(1), [self.x[1]]), ("rxz", lambda: self.step2(2), [self.x[2]]))

        def step1(self):
            self.y.wait_recv()
            for c in self.x:
                go(c)
            go(self.f[0])

        def step2(self, i):
            self.x[i].wait_recv()
            go(self.f[i + 1])

        def near(self):
            self.loc.wait()
            self.c.wait_recv()

        def ready(self):
            for c in self.f:
                c.wait_recv()

    w_qkv = Gather("qkv")
    w_o = Gather("wo")
    w_up = Gather("up")
    w_dn = Gather("dn")
    live("qkv", "wo", "up", "dn")

    for i, ref in enumerate((v0_in, v1_in, v2_in, v3_in, v4_in, v5_in)):
        vec[i:i + 1, :] = ref[...].reshape(1, D)

    def row(i):
        return vec[i:i + 1, :]

    load_x.wait()

    class Halo:
        def __init__(self, pairs):
            self.left = [remote(a, b, (r, (t + 3) % 4)) for a, b, _, _ in pairs]
            self.right = [remote(c, d, (r, (t + 1) % 4)) for _, _, c, d in pairs]

        def send(self, i):
            pl.when(t > 0)(self.left[i].start)
            pl.when(t < 3)(self.right[i].start)

        def wait(self, i):
            pl.when(t > 0)(self.right[i].wait_recv)
            pl.when(t < 3)(self.left[i].wait_recv)

        def sent(self):
            for i in range(2):
                pl.when(t > 0)(self.left[i].wait_send)
                pl.when(t < 3)(self.right[i].wait_send)

    HR = RH // 2

    def edges(i, first):
        return nw.at[pl.ds(i * HR, HR), pl.ds(first, HALO)]

    halo = Halo([(edges(i, HALO), edges(i, HALO + LS), edges(i, LS), edges(i, 0)) for i in range(2)])

    def ln1(b):
        xs = x[pl.ds(b * BT, BT), :].astype(F32)
        unit, _ = normalize(xs)
        out = (unit * row(1) + row(2)).astype(BF)
        nw[pl.ds(b * BR, BR), HALO:HALO + LS, :] = out.reshape(BR, LS, D)

    run("ln1", NB, ln1, {NB // 2 - 1: lambda: halo.send(0), NB - 1: lambda: halo.send(1)})

    @pl.when(t == 0)
    def _():
        nw[:, 0:HALO, :] = jnp.zeros((RH, HALO, D), BF)

    @pl.when(t == 3)
    def _():
        nw[:, HALO + LS:W, :] = jnp.zeros((RH, HALO, D), BF)

    PH = RH * SEGS // 2
    load_wp.wait()
    load_eg.wait()

    class PoolSum:
        def __init__(self, name, terms, r1, r2, out):
            self.terms, self.r1, self.r2, self.out = terms, r1, r2, out
            mine, theirs = pl.ds(core * PH, PH), pl.ds((1 - core) * PH, PH)
            self.mine = mine
            self.a = remote(terms.at[theirs], r1, (r, tc))
            self.b = remote(terms.at[mine], r2, (r, ty))
            self.c = remote(out.at[mine], out.at[mine], (r, tc))
            chain(name, ("step2", self.step2, [self.a]), ("step3", self.step3, [self.b]))

        def step1(self):
            go(self.a)

        def step2(self):
            self.a.wait_recv()
            self.terms[self.mine, :] = (self.terms[self.mine, :].astype(F32) + self.r1[...].astype(F32)).astype(BF)
            go(self.b)

        def step3(self):
            self.b.wait_recv()
            self.out[self.mine, :] = (self.terms[self.mine, :].astype(F32) + self.r2[...].astype(F32)).astype(BF)
            go(self.c)

        def ready(self):
            self.c.wait_recv()

    gpool = PoolSum("gpool", gpt, gpr1, gpr2, gps)
    pooled = PoolSum("pooled", pt, pr1, pr2, ps)
    smalls[...] = jnp.zeros(smalls.shape, F32)

    def pool_back():
        smalls[pl.ds(12 + t, 1), :] = total(eg[...].astype(F32))
        gpt[...] = mm_t(eg[...], wp[...]).astype(BF)

    once("pool_back", pool_back)
    gpool.step1()

    load_hg = local(hg_in, hg)
    w_qkv.near()
    live("gpool")
    point()

    labels = lab_in[...]
    SL = labels.shape[1]
    window = pltpu.roll(labels, (SL + HALO - t * LS) % SL, 1)[:, 0:W].astype(F32)
    own_lab = pltpu.roll(labels, (SL - t * LS) % SL, 1)[:, 0:W].astype(F32)
    before = pltpu.roll(labels, (SL + 1 - t * LS) % SL, 1)[:, 0:W].astype(F32)
    codes[...] = jnp.where(own_lab == before, -1.0, own_lab)
    columns = jnp.transpose(own_lab)
    for i in range(RH):
        mask[i * LS:(i + 1) * LS, :] = jnp.where(columns[0:LS, i:i + 1] == window[i:i + 1, :], 0.0, -1e30)

    for copy in bias_moves:
        copy.wait_recv()
    for s in range(4):
        for i in range(2):
            vec[6 + i:7 + i, s * 128:(s + 1) * 128] = shared[s, i:i + 1, :]
        for i in range(4):
            bup[s:s + 1, i * 128:(i + 1) * 128] = shared[s, 2 + i:3 + i, :]

    point()

    near = pl.ds(pl.multiple_of(ypos * H2, H2), H2)
    far = pl.ds(pl.multiple_of((1 - ypos) * H2, H2), H2)

    def project_own(cols, b):
        own = nw[pl.ds(b * BR, BR), HALO:HALO + LS, :].reshape(BT, D)
        q[pl.ds(b * BT, BT), cols] = ((mm(own, wqkv[0, :, cols]) + vec[6:7, cols]) * (HEAD_DIM ** -0.5)).astype(BF)
        ks = mm(own, wqkv[1, :, cols]).astype(BF)
        vs = (mm(own, wqkv[2, :, cols]) + vec[7:8, cols]).astype(BF)
        k[pl.ds(b * BR, BR), HALO:HALO + LS, cols] = ks.reshape(BR, LS, H2)
        v[pl.ds(b * BR, BR), HALO:HALO + LS, cols] = vs.reshape(BR, LS, H2)

    def project_halo(b):
        rows_ = pl.ds(b * BR, BR)
        both = jnp.concatenate([nw[rows_, 0:HALO, :], nw[rows_, HALO + LS:W, :]], axis=0).reshape(BR * 2 * HALO, D)
        ks = mm(both, wqkv[1]).astype(BF).reshape(2, BR, HALO, D)
        vs = (mm(both, wqkv[2]) + row(7)).astype(BF).reshape(2, BR, HALO, D)
        k[rows_, 0:HALO, :] = ks[0]
        k[rows_, HALO + LS:W, :] = ks[1]
        v[rows_, 0:HALO, :] = vs[0]
        v[rows_, HALO + LS:W, :] = vs[1]

    lane = lax.broadcasted_iota(jnp.int32, (1, H2), 1) // HEAD_DIM
    heads = [(lane == h).astype(F32).astype(BF) for h in range(4)]

    def spread_heads(block):
        return jnp.concatenate([block * heads[h] for h in range(4)], axis=0)

    def merge_heads(stack):
        parts = [stack[h * LS:(h + 1) * LS, :] for h in range(4)]
        out = jnp.where(lane == 0, parts[0], parts[1])
        out = jnp.where(lane == 2, parts[2], out)
        return jnp.where(lane == 3, parts[3], out)

    def attend(i):
        work = [(i * 2 + n, half) for n in range(2) for half in range(2)]
        sides = [slice(half * H2, (half + 1) * H2) for _, half in work]
        scores = []
        for (n, _), c in zip(work, sides):
            m1 = mask[pl.ds(n * LS, LS), :]
            qs = spread_heads(q[pl.ds(n * LS, LS), c])
            scores.append(mm_t(qs, k[n, :, c]) + jnp.concatenate([m1] * 4, axis=0))
        tops = [jnp.max(sc, axis=-1, keepdims=True) for sc in scores]
        es = [jnp.exp(sc - top) for sc, top in zip(scores, tops)]
        inv = [1.0 / jnp.sum(e, axis=-1, keepdims=True) for e in es]
        ws = [(e * f).astype(BF) for e, f in zip(es, inv)]
        outs = []
        for (n, half), c, w in zip(work, sides, ws):
            p[pl.ds((n * 2 + half) * 4 * LS, 4 * LS), :] = w
            outs.append(mm(w, v[n, :, c]))
        for (n, _), c, o in zip(work, sides, outs):
            at[pl.ds(n * LS, LS), c] = merge_heads(o).astype(BF)

    HB = NB // 2
    AB = RH // 4
    run("own_near", NB, lambda b: project_own(near, b))
    must("qkv")
    w_qkv.ready()
    run("own_far", NB, lambda b: project_own(far, b))
    halo.wait(0)
    run("halo_all", HB, project_halo)
    run("attend", AB, attend)
    halo.wait(1)
    run("halo_all", HB, lambda b: project_halo(b + HB))
    run("attend", AB, lambda i: attend(i + AB))
    must("wo", "up", "dn")
    for w in (w_o, w_up, w_dn):
        w.near()
        w.ready()

    FC = FF // 4
    ids = lax.broadcasted_iota(jnp.int32, (SEGS, LS), 0).astype(F32)

    def chosen(n):
        return (ids == codes[pl.ds(n, 1), 0:LS]).astype(F32).astype(BF)

    def feed(b):
        rows_ = pl.ds(b * BT, BT)
        middle = x[rows_, :].astype(F32) + (mm(at[rows_, :], wo[...]) + row(0))
        mid[rows_, :] = middle
        unit, _ = normalize(middle)
        normed = (unit * row(3) + row(4)).astype(BF)
        nf[rows_, :] = normed
        acc = middle + row(5)
        for j in range(4):
            cols = slice(j * FC, (j + 1) * FC)
            u = mm(normed, wup[:, cols]) + bup[j:j + 1, :]
            u2 = u * u
            th = jnp.tanh(ROOT * u * (1.0 + CUBE * u2))
            half_up = 0.5 * (1.0 + th)
            a = (u * half_up).astype(BF)
            act[rows_, cols] = a
            dact[rows_, cols] = (half_up + u * half_up * (1.0 - th) * (ROOT + (3.0 * CUBE * ROOT) * u2)).astype(BF)
            acc = acc + mm(a, wdn[cols, :])
        low = acc.astype(BF)
        hid[rows_, :] = low
        for n in range(BR):
            first = chosen(b * BR + n)
            pt[pl.ds((b * BR + n) * SEGS, SEGS), :] = mm(first, low[n * LS:(n + 1) * LS, :]).astype(BF)

    run("feed", NB, feed)
    store_hid = local(hid, hid_out)
    pooled.step1()
    live("pooled")
    must("gpool")
    gpool.ready()
    load_hg.wait()

    def place(b):
        rows_ = pl.ds(b * BT, BT)
        put = [t_mm(chosen(b * BR + n), gps[pl.ds((b * BR + n) * SEGS, SEGS), :]) for n in range(BR)]
        g = hg[rows_, :].astype(F32) + jnp.concatenate(put, axis=0)
        low = g.astype(BF)
        hg[rows_, :] = low
        smalls[5:6, :] += total(low.astype(F32))

    run("place", NB, place)
    gb = hg

    class Reduce:
        def __init__(self, name, g, r1, r2, r3, r4, o):
            self.name, self.g, self.r1, self.r2, self.r3, self.r4, self.o = name, g, r1, r2, r3, r4, o
            own = g
            if r1 is not None:
                self.a1 = remote(g.at[1 - core, 1 - ypos], r1.at[1 - ypos], (r, tc))
                self.a2 = remote(g.at[1 - core, ypos], r1.at[ypos], (r, tc))
                own = g.at[core, ypos]
            self.own = own
            self.middle()
            self.d = [remote(own.at[(zpos + dz) % 4, xpos], r4.at[dz - 1], (zpeers[dz - 1], t)) for dz in (1, 2, 3)]
            if groups > 1:
                self.m = [remote(o.at[zpos, xpos], r5[name].at[i], (gpeers[i], t)) for i in range(groups - 1)]
            self.e = [remote(o.at[zpos, xpos], o.at[zpos, xpos], (zpeers[dz - 1], t)) for dz in (1, 2, 3)]
            self.f = remote(o.at[:, xpos], o.at[:, xpos], (rx, t))
            ends = [("gz", self.gather_z, self.d), ("gx", self.gather_x, self.e), ("end", self.finish, [self.f])]
            chain(name, *self.links(), *ends)

        def links(self):
            if self.r1 is None:
                return [("x", self.x, []), ("z", self.z, [self.c])]
            return [("y", self.y, [self.a1]), ("x", self.x, [self.a2, self.b]), ("z", self.z, [self.c])]

        def middle(self):
            if self.r1 is not None:
                self.b = remote(self.g.at[core, 1 - ypos], self.r2, (r, ty))
            self.c = remote(self.own.at[:, 1 - xpos], self.r3, (rx, t))

        def core1(self):
            go(self.a1)

        def core2(self):
            go(self.a2)

        def y(self):
            self.a1.wait_recv()
            self.g[core, 1 - ypos] = (self.g[core, 1 - ypos].astype(F32) + self.r1[1 - ypos].astype(F32)).astype(BF)
            go(self.b)

        def part(self, i):
            acc = self.own[:, i].astype(F32)
            if self.r1 is not None:
                acc = acc + self.r1[ypos, :, i].astype(F32) + self.r2[:, i].astype(F32)
            return acc

        def x(self):
            if self.r1 is not None:
                self.a2.wait_recv()
                self.b.wait_recv()
                self.own[:, 1 - xpos] = self.part(1 - xpos).astype(BF)
            go(self.c)

        def z(self):
            self.c.wait_recv()
            self.own[:, xpos] = (self.part(xpos) + self.r3[...].astype(F32)).astype(BF)
            for c in self.d:
                go(c)

        def gather_z(self):
            for c in self.d:
                c.wait_recv()
            acc = self.own[zpos, xpos].astype(F32)
            for i in range(3):
                acc = acc + self.r4[i].astype(F32)
            self.o[zpos, xpos] = acc.astype(BF)
            if groups > 1:
                for c in self.m:
                    c.start()
                for c in self.m:
                    c.wait()
                acc = self.o[zpos, xpos].astype(F32)
                for i in range(groups - 1):
                    acc = acc + r5[self.name][i].astype(F32)
                self.o[zpos, xpos] = acc.astype(BF)
            for c in self.e:
                go(c)

        def gather_x(self):
            for c in self.e:
                c.wait_recv()
            go(self.f)

        def finish(self):
            self.f.wait_recv()
            stores.append(local(self.o, final[self.name]))

    class ReduceX(Reduce):
        def links(self):
            return [("x", self.x, [self.a1, self.a2]), ("y", self.y, [self.c]), ("z", self.z, [self.b])]

        def middle(self):
            self.c = remote(self.g.at[core, :, :, 1 - xpos], self.r3, (rx, t))
            self.b = remote(self.g.at[core, 1 - ypos, :, xpos], self.r2, (r, ty))

        def x(self):
            self.a1.wait_recv()
            self.a2.wait_recv()
            both = self.g[core, :, :, 1 - xpos].astype(F32) + self.r1[:, :, 1 - xpos].astype(F32)
            self.g[core, :, :, 1 - xpos] = both.astype(BF)
            go(self.c)

        def half(self, i):
            return self.g[core, i, :, xpos].astype(F32) + self.r1[i, :, xpos].astype(F32) + self.r3[i].astype(F32)

        def y(self):
            self.c.wait_recv()
            self.g[core, 1 - ypos, :, xpos] = self.half(1 - ypos).astype(BF)
            go(self.b)

        def z(self):
            self.b.wait_recv()
            self.g[core, ypos, :, xpos] = (self.half(ypos) + self.r2[...].astype(F32)).astype(BF)
            for c in self.d:
                go(c)

    HC = D // 2

    def halves(out, i):
        return out.at[:, :, :, pl.ds(i * HC, HC)]

    final = {"dna": halves(gdn_out, 0), "dnb": halves(gdn_out, 1), "upa": halves(gup_out, 0), "upb": halves(gup_out, 1),
             "o": go_out, "q": gq_out, "k": gk_out, "v": gv_out, "pl": gpl_out}
    stores = []
    red = {}
    for name in NAMES:
        held = sets[name]
        if name == "pl":
            held = [held[0], None, None] + held[1:]
        red[name] = (ReduceX if name in X_FIRST else Reduce)(name, *held)

    def split(names, cs, ys, val):
        for i, name in enumerate(names):
            g = sets[name][0]
            g[cs, ys] = val[:, i * HC:(i + 1) * HC].astype(BF).reshape(g.shape[2:])

    def place_of(i):
        return (core + 1 + i // 2) % 2, (ypos + 1 + i) % 2

    def down_grad(i):
        cs, ys = place_of(i)
        val = t_mm(act[:, pl.ds(pl.multiple_of((ys * 2 + cs) * FC, FC), FC)], gb[...])
        split(("dna", "dnb"), cs, ys, val)

    def near_cores(*names):
        return lambda: [red[n].core1() for n in names], lambda: [red[n].core2() for n in names]

    send1, send2 = near_cores("dna", "dnb")
    run("down_grad", 4, down_grad, {0: send1, 1: send2, 2: lambda: live("dnb"), 3: lambda: live("dna")})

    def feed_back(b):
        rows_ = pl.ds(b * BT, BT)
        g = gb[rows_, :]
        acc = jnp.zeros((BT, D), F32)
        for j in range(4):
            cols = slice(j * FC, (j + 1) * FC)
            ga = mm_t(g, wdn[cols, :])
            gp = (ga * dact[rows_, cols].astype(F32)).astype(BF)
            dact[rows_, cols] = gp
            smalls[8 + j:9 + j, :] += total(gp.astype(F32))
            acc = acc + mm_t(gp, wup[:, cols])
        unit, factor = normalize(mid[rows_, :])
        smalls[3:4, :] += total(acc * unit)
        smalls[4:5, :] += total(acc)
        gm = g.astype(F32) + norm_back(acc, unit, factor, row(3))
        mid[rows_, :] = gm
        low = gm.astype(BF)
        gma[rows_, :] = low
        smalls[0:1, :] += total(low.astype(F32))
        gat[rows_, :] = mm_t(low, wo[...]).astype(BF)

    run("feed_back", NB, feed_back)
    must("pooled")
    pooled.ready()

    def embed():
        emb[...] = (mm(ps[...], wp[...]) + bp_in[...].reshape(1, D)).astype(BF)
        sets["pl"][0][...] = t_mm(ps[...], eg[...]).astype(BF).reshape(sets["pl"][0].shape)
        live("pl")

    once("embed", embed)
    store_emb = local(emb, emb_out)

    def up_grad(i):
        cs, ys = place_of(i)
        val = t_mm(nf[...], dact[:, pl.ds(pl.multiple_of((ys * 2 + cs) * FC, FC), FC)])
        split(("upa", "upb"), cs, ys, val)

    send3, send4 = near_cores("upa", "upb")
    run("up_grad", 4, up_grad, {0: send3, 1: send4, 2: lambda: live("upb"), 3: lambda: live("upa")})

    def out_grad():
        val = t_mm(at[...], gma[...]).astype(BF)
        for s in range(4):
            g = sets["o"][0]
            g[s % 2, s // 2] = val[s * (D // 4):(s + 1) * (D // 4), :].reshape(g.shape[2:])
        red["o"].core1()
        red["o"].core2()
        live("o")

    once("out_grad", out_grad)

    def attend_back(i):
        work = [(i * 2 + n, half) for n in range(2) for half in range(2)]
        sides = [slice(half * H2, (half + 1) * H2) for _, half in work]
        qss = [spread_heads(q[pl.ds(n * LS, LS), c]) for (n, _), c in zip(work, sides)]
        gss = [spread_heads(gat[pl.ds(n * LS, LS), c]) for (n, _), c in zip(work, sides)]
        ws = [p[pl.ds((n * 2 + half) * 4 * LS, 4 * LS), :] for n, half in work]
        gws = [mm_t(g, v[n, :, c]) for g, (n, _), c in zip(gss, work, sides)]
        wfs = [w.astype(F32) for w in ws]
        prods = [w * g for w, g in zip(wfs, gws)]
        sums = [jnp.sum(pr, axis=-1, keepdims=True) for pr in prods]
        dss = [(pr - w * sm).astype(BF) for pr, w, sm in zip(prods, wfs, sums)]
        dvs = [t_mm(w, g).astype(BF) for w, g in zip(ws, gss)]
        dqs = [mm(ds, k[n, :, c]) for ds, (n, _), c in zip(dss, work, sides)]
        dks = [t_mm(ds, qq).astype(BF) for ds, qq in zip(dss, qss)]
        for (n, _), c, dq, dk, dv in zip(work, sides, dqs, dks, dvs):
            q[pl.ds(n * LS, LS), c] = (merge_heads(dq) * (HEAD_DIM ** -0.5)).astype(BF)
            k[n, :, c] = dk
            v[n, :, c] = dv

    run("attend_back", RH // 2, attend_back)

    back = Halo([tuple(ref.at[pl.ds(i * HR, HR)] for ref in (halo_l, halo_fr, halo_r, halo_fl)) for i in range(2)])

    def norm_grad(b):
        keys = pl.ds(b * BR, BR)
        dqs = q[pl.ds(b * BT, BT), :]
        dks, dvs = k[keys].reshape(BR * W, D), v[keys].reshape(BR * W, D)
        smalls[6:7, :] += total(dqs.astype(F32))
        smalls[7:8, :] += total(dvs.astype(F32))
        win = (mm_t(dks, wqkv[1]) + mm_t(dvs, wqkv[2])).reshape(BR, W, D)
        own = win[:, HALO:HALO + LS, :].reshape(BT, D) + mm_t(dqs, wqkv[0])
        gnc[pl.ds(b * BT, BT), :] = own
        halo_l[keys] = win[:, 0:HALO, :].astype(BF)
        halo_r[keys] = win[:, HALO + LS:W, :].astype(BF)

    def put_at(g, val):
        low = val.astype(BF)
        for s in range(4):
            g[s % 2, s // 2] = low[:, s * 128:(s + 1) * 128].reshape(g.shape[2:])

    def put_value():
        put_at(sets["v"][0], t_mm(nw[...].reshape(RH * W, D), v[...].reshape(RH * W, D)))
        red["v"].core1()
        red["v"].core2()
        live("v")

    def put_key():
        put_at(sets["k"][0], t_mm(nw[...].reshape(RH * W, D), k[...].reshape(RH * W, D)))
        red["k"].core1()
        red["k"].core2()
        live("k")

    def put_query():
        put_at(sets["q"][0], t_mm(nw[:, HALO:HALO + LS, :].reshape(T, D), q[...]))
        red["q"].core1()
        red["q"].core2()
        live("q")

    once("put_v", put_value)
    once("put_k", put_key)
    once("put_q", put_query)
    run("norm_grad", NB, norm_grad, {HB - 1: lambda: back.send(0), NB - 1: lambda: back.send(1)})

    @pl.when(t == 0)
    def _():
        halo_fl[...] = jnp.zeros(halo_fl.shape, BF)

    @pl.when(t == 3)
    def _():
        halo_fr[...] = jnp.zeros(halo_fr.shape, BF)

    class Small:
        name = "sm"

        def __init__(self):
            self.copies = [[remote(smalls, sm_r.at[0], (r, tc))], [remote(smalls, sm_r.at[1], (r, ty))],
                           [remote(smalls, sm_r.at[2], (rx, t))],
                           [remote(smalls, sm_r.at[2 + dz], (zpeers[dz - 1], t)) for dz in (1, 2, 3)]]
            chain("sm", *[("s" + str(i), functools.partial(self.step, i), self.copies[i]) for i in range(4)])

        def send(self, i):
            for c in self.copies[i]:
                c.start()

        def step(self, i):
            for c in self.copies[i]:
                c.wait()
            if i < 3:
                smalls[...] += sm_r[i]
                self.send(i + 1)
            else:
                smalls[...] += sm_r[3] + sm_r[4] + sm_r[5]
                across(smalls, "sm")
                stores.append(local(smalls, sm_out))

    class Late:
        name = "late"

        def __init__(self):
            self.a = [remote(late, late_tp.at[i], (r, dev)) for i, dev in enumerate((tc, ty, tdiag))]
            self.b = [remote(late, late_rows.at[i], (dev, t)) for i, dev in enumerate([rx] + zpeers + xzpeers)]
            chain("late", ("tp", self.over_tp, self.a), ("rows", self.over_rows, self.b))

        def over_tp(self):
            for c in self.a:
                c.wait()
            late[...] += late_tp[0] + late_tp[1] + late_tp[2]
            for c in self.b:
                c.start()

        def over_rows(self):
            for c in self.b:
                c.wait()
            for i in range(7):
                late[...] += late_rows[i]
            across(late, "late")
            stores.append(local(late, late_out))

    def across(ref, name):
        moves = [remote(ref, r5[name].at[i], (gpeers[i], t)) for i in range(groups - 1)]
        for c in moves:
            c.start()
        for c in moves:
            c.wait()
        for i in range(groups - 1):
            ref[...] += r5[name][i]

    small, lates = Small(), Late()
    small.send(0)
    live("sm")
    late[...] = jnp.zeros(late.shape, F32)

    def ln1_back(b):
        rows_ = pl.ds(b * BT, BT)
        grp = pl.ds(b * BR, BR)
        g = gnc[rows_, :].reshape(BR, LS, D)
        g = jnp.concatenate([g[:, 0:HALO, :] + halo_fl[grp].astype(F32), g[:, HALO:LS, :] + halo_fr[grp].astype(F32)], axis=1)
        g = g.reshape(BT, D)
        unit, factor = normalize(x[rows_, :].astype(F32))
        late[0:1, :] += total(g * unit)
        late[1:2, :] += total(g)
        nf[rows_, :] = (mid[rows_, :] + norm_back(g, unit, factor, row(1))).astype(BF)

    back.wait(0)
    run("ln1_back", HB, ln1_back)
    back.wait(1)
    run("ln1_back", HB, lambda b: ln1_back(b + HB))
    store_ig = local(nf, ig_out)
    for c in lates.a:
        c.start()
    live("late")
    must(*NAMES, "sm", "late")
    for c in pending:
        c.wait_send()
    halo.sent()
    back.sent()
    for c in stores + [store_hid, store_emb, store_ig]:
        c.wait()


def per_device(rows_size, layer_input, segment_labels, attend_weight, attend_bias, out_weight, out_bias, gain_attention,
               shift_attention, gain_feed, shift_feed, up_weight, up_bias, down_weight, down_bias, pool_weight, pool_bias,
               hidden_grad, embedding_grad):
    RH, LS, D = layer_input.shape
    SEGS = embedding_grad.shape[1]
    OC = pool_weight.shape[1]
    FS = up_weight.shape[1]
    FF = FS * 4
    W = LS + 2 * HALO
    T = RH * LS
    NB = RH // 4
    groups = rows_size // 8
    t = lax.axis_index("tp")
    part = (D // 8, D // 4)
    chunk = {"dna": (FS // 8, D // 2), "dnb": (FS // 8, D // 2), "upa": (D // 8, FS // 2), "upb": (D // 8, FS // 2), "o": (D // 32, D), "q": part, "k": part, "v": part, "pl": (D // 8, OC)}
    any_, vmem = pl.BlockSpec(memory_space=pl.ANY), pl.BlockSpec(memory_space=pltpu.VMEM)

    def buf(*shape, dtype=BF):
        return pltpu.VMEM(shape, dtype)

    scratch = [
        buf(T, D), buf(T, D), buf(RH * SEGS, OC), buf(T, W, dtype=F32), buf(RH, W, dtype=F32),
        buf(3, D, D), buf(D, D), buf(D, FF), buf(FF, D), buf(D, OC), buf(4, 8, 128, dtype=F32), buf(8, D, dtype=F32), buf(4, FS, dtype=F32),
        buf(RH, W, D), buf(T, D), buf(RH, W, D), buf(RH, W, D), buf(RH * 2 * 4 * LS, W), buf(T, D), buf(T, D, dtype=F32),
        buf(T, D), buf(T, FF), buf(T, FF), buf(T, D), buf(T, D), buf(T, D), buf(T, D, dtype=F32),
        buf(RH, HALO, D), buf(RH, HALO, D), buf(RH, HALO, D), buf(RH, HALO, D),
    ]
    for _ in range(2):
        scratch += [buf(RH * SEGS, D), buf(RH * SEGS // 2, D), buf(RH * SEGS // 2, D), buf(RH * SEGS, D)]
    scratch += [buf(RH * SEGS, OC), buf(16, D, dtype=F32), buf(6, 16, D, dtype=F32), buf(2, D, dtype=F32), buf(3, 2, D, dtype=F32), buf(7, 2, D, dtype=F32)]
    for name in NAMES[:-1]:
        c = chunk[name]
        steps = [buf(4, *c), buf(2, 4, *c)] if name in X_FIRST else [buf(4, 2, *c), buf(4, *c)]
        scratch += [buf(2, 2, 4, 2, *c), buf(2, 4, 2, *c)] + steps + [buf(3, *c), buf(4, 2, *c)]
    c = chunk["pl"]
    scratch += [buf(4, 2, *c), buf(4, *c), buf(3, *c), buf(4, 2, *c)]
    if groups > 1:
        scratch += [buf(groups - 1, *chunk[name]) for name in NAMES]
        scratch += [buf(groups - 1, 16, D, dtype=F32), buf(groups - 1, 2, D, dtype=F32)]
    n_remote = 4 * 9 + 3 + 8 + 6 + 9 * 11 + 6 + 10 + 11 * (groups - 1)
    scratch += [pltpu.SemaphoreType.DMA((n_remote,)), pltpu.SemaphoreType.DMA((n_remote,)), pltpu.SemaphoreType.DMA((24,))]

    def out(*shape, dtype=BF):
        return jax.ShapeDtypeStruct(shape, dtype)

    flops = 30 * T * D * FF
    hid, emb, ig, gdn, gup, go_, gq, gk, gv, gpl, sm, late = pl.pallas_call(
        functools.partial(layer_kernel, (groups, RH, LS, D, FF, SEGS)),
        out_shape=[out(T, D), out(RH * SEGS, OC), out(T, D)]
        + [out(4, 2, FS // 8, D), out(4, 2, D // 8, FS)] + [out(4, 2, *chunk[name]) for name in ("o", "q", "k", "v", "pl")]
        + [out(16, D, dtype=F32), out(2, D, dtype=F32)],
        in_specs=[any_, vmem, any_, vmem, any_] + [vmem] * 5 + [any_, vmem, any_, vmem, any_, vmem, any_, any_],
        out_specs=[any_] * 12,
        scratch_shapes=scratch,
        compiler_params=pltpu.CompilerParams(collective_id=0, has_side_effects=True, vmem_limit_bytes=63 * 2 ** 20),
        cost_estimate=pl.CostEstimate(flops=flops, bytes_accessed=20 * 2 ** 20, transcendentals=T * FF),
        name="layer",
    )(layer_input.reshape(T, D), segment_labels, attend_weight, attend_bias, out_weight, out_bias, gain_attention,
      shift_attention, gain_feed, shift_feed, up_weight, up_bias.reshape(4, FS // 4), down_weight, down_bias,
      pool_weight, pool_bias, hidden_grad.reshape(T, D), embedding_grad.reshape(RH * SEGS, OC))

    d8 = D // 4
    return (
        hid.reshape(RH, LS, D),
        emb.reshape(RH, SEGS, OC),
        ig.reshape(RH, LS, D),
        jnp.stack([gq, gk, gv]).reshape(3, D, D // 4).astype(F32),
        lax.dynamic_slice_in_dim(sm[6:8], t * d8, d8, 1),
        go_.reshape(D // 4, D).astype(F32),
        sm[0], late[0], late[1], sm[3], sm[4],
        gup.reshape(D, FS).astype(F32),
        lax.dynamic_slice_in_dim(sm, 8 + t, 1, 0)[0],
        gdn.reshape(FS, D).astype(F32),
        sm[5],
        gpl.reshape(D, OC).astype(F32),
        lax.dynamic_slice_in_dim(sm, 12 + t, 1, 0)[0],
    )


def solution(mesh):
    placed = (
        P("rows", "tp", None), P("rows", None), P(None, None, "tp"), P(None, "tp"), P("tp", None), P(), P(), P(), P(), P(),
        P(None, "tp"), P("tp"), P("tp", None), P(), P(None, "tp"), P("tp"), P("rows", "tp", None), P("rows", None, "tp"),
    )
    return jax.shard_map(
        functools.partial(per_device, mesh.shape["rows"]),
        mesh=mesh,
        in_specs=placed,
        out_specs=(
            P("rows", "tp", None), P("rows", None, "tp"), P("rows", "tp", None), P(None, None, "tp"), P(None, "tp"),
            P("tp", None), P(), P(), P(), P(), P(), P(None, "tp"), P("tp"), P("tp", None), P(), P(None, "tp"), P("tp"),
        ),
        check_vma=False,
    )
```

time: 776 us -> 136 us (0.18); the launches traced: 767 us -> 136 us
  waiting for transfers between devices: 460 us -> 0 us
  matrix products: 168 us -> 0 us
  Pallas kernels: 0 us -> 123 us
  blocking collectives: 63.6 us -> 0 us
  other arithmetic: 30.1 us -> 5.61 us
  local copies, waits for them, and re-layouts: 27.9 us -> 6.58 us
  between operations: 15.1 us -> 0.7 us
    reduce_scatter x4 -> x0, waiting for transfers between devices: 174 us -> none  [the longest x1 44.6 us: per_device(): lax.psum_scatter(feed_back_terms.astype(jnp.bfloat16), 'tp', scatter_dime...]
    dot_general x73 -> x0, matrix products: 168 us -> none  [the longest x16 22.5 us: head_scores(): jnp.einsum('bqhd,bkhd->bhqk', query_block, key_block, preferred_element_t...]
    psum x2 -> x0, waiting for transfers between devices: 158 us -> none  [the longest x1 122 us: per_device(): lax.psum((attend_weight_grad, attend_bias_grad, out_weight_grad, up_weigh...]
    all_gather x4 -> x0, waiting for transfers between devices: 128 us -> none  [the longest x2 71.7 us: per_device(): norm_full = lax.all_gather(normed, 'tp', axis=1, tiled=True)]
    pallas_call x0 -> x1, Pallas kernels: none -> 123 us  [per_device(): pl.pallas_call(functools.partial(layer_kernel, (groups, RH, LS, D, FF, SE...]
    psum x2 -> x0, blocking collectives: 63.6 us -> none  [the longest x1 39.6 us: per_device(): lax.psum((out_bias_grad, gain_attention_grad, shift_attention_grad, gain_...]
    reduce_sum x19 -> x0, other arithmetic: 18.5 us -> none  [the longest x4 7.74 us: layer_norm(): return centred * lax.rsqrt(spread_sq + epsilon) * gain + shift]
    another operation x8 -> x0, local copies, waits for them, and re-layouts: 11.2 us -> none  [the longest x3 6.78 us: per_device(): jnp.stack([grad_queries, grad_keys, grad_values])]
  transfers between devices with their start and end apart: 10 -> 0, of which waited for: 10 -> 0; matrix products, arithmetic and copies ran while one was open for 4% -> 0% of each run, Pallas kernels for 0% -> 0%
where the time goes in v1:
time: 136 us
  Pallas kernels  123 us (90%)
  local copies, waits for them, and re-layouts  6.58 us (5%)
  other arithmetic  5.61 us (4%)
    pallas_call x1, Pallas kernels, per_device(): pl.pallas_call(functools.partial(layer_kernel, (groups, RH, LS, D, FF, SE...  123 us
    unnamed x17, local copies, waits for them, and re-layouts  3.8 us

profile of v1, /device:TPU:0, one launch (start us, length us, event | category | flops | bytes accessed | tf_op | source)
XLA Modules:
  0.0 136.0 jit_solution(16206112042803861175)
XLA Ops:
  0.7 123.2 %layer.1 = (bf16[1024,512]{1,0:T(8,128)(2,1)}, bf16[512,512]{1,0:T(8,128)(2,1)}, bf16[1024,512]{1,0:T(8,128)(2,1)}, bf16[4,2,64,512]{3,2,1,0:T(8,128)(2,1)}, bf1...) custom-call(bf16[1024,512]{1,0:T(8,128)(2,1)} %bitcast.44, ...), custom_call_target="tpu_custom_call" | custom-call | flops 32212254720 | bytes 20971520 | tf_op jit(solution)/shard_map/layer/pallas_call | solution.py:948
  123.8 1.5 %constant_dynamic-slice_fusion = (f32[1,512]{1,0:T(1,128)}, f32[1,512]{1,0:T(1,128)}, f32[1,512]{1,0:T(1,128)}, f32[1,512]{1,0:T(1,128)}, f32[1,512]{1,0:T(1,128...) fusion(f32[16,512]{1,0:T(8,128)} %get-tuple-element.35, s32[]{:T(128)S(6)} %select_n.11, s32[]{:T(128)S(6)} %select_n.10, ...), kind=kLoop, calls=%fused_computation.5 | loop fusion | bytes 32776 | tf_op jit(solution)/shard_map/dynamic_slice | solution.py:977
  125.3 0.0 copy-start.4
  125.3 0.0 copy-start.5
  125.3 2.1 %maximum_convert_fusion = f32[3,512,128]{2,1,0:T(8,128)} fusion(bf16[1,512,128]{2,1,0:T(8,128)(2,1)} %bitcast.35, bf16[1,512,128]{2,1,0:T(8,128)(2,1)} %bitcast.34, bf16[1,512,128]{2,1,0:T(8,128)(2,1)} %bitcast.33), kind=kLoop, calls=%fused_computation.3 | loop fusion | flops 589824 | bytes 1179648 | tf_op jit(solution)/shard_map/convert_element_type | solution.py:968
  127.4 0.7 slice.21
  128.1 0.6 constant_dynamic-slice_fusion.2
  128.7 0.0 copy-done.4
  128.7 0.0 copy-done.5
  128.7 0.0 copy-start.2
  128.7 1.7 %bitcast_convert_fusion = (f32[512,512]{1,0:T(8,128)}, f32[512,512]{1,0:T(8,128)}) fusion(bf16[4,2,64,512]{3,2,1,0:T(8,128)(2,1)S(1)} %copy-done.5, bf16[4,2,64,512]{3,2,1,0:T(8,128)(2,1)S(1)} %copy-done.4), kind=kLoop, calls=%fused_computation | loop fusion | flops 524288 | bytes 3145728 | tf_op jit(solution)/shard_map/convert_element_type | solution.py:976
  130.4 0.0 copy-start.1
  130.4 0.0 copy-done.2
  130.4 0.0 copy-start.6
  130.4 1.1 bitcast_convert_fusion.2
  131.5 0.0 copy-done.6
  131.5 0.7 bitcast_convert_fusion.3
  132.2 0.0 copy-done.1
  132.3 0.0 copy-start.3
  132.3 1.0 copy.38
  133.2 0.4 copy-done.3
  133.7 0.0 copy-start
  133.7 0.8 copy.39
  134.4 0.6 copy-done
  135.1 1.0 copy.40
Async XLA Ops:
  125.3 3.4 %copy-start.4 = (bf16[4,2,64,512]{3,2,1,0:T(8,128)(2,1)S(1)}, bf16[4,2,64,512]{3,2,1,0:T(8,128)(2,1)}, u32[]{:S(2)}) copy-start(bf16[4,2,64,512]{3,2,1,0:T(8,128)(2,1)} %get-tuple-element.39) | copy-start | bytes 1572868
  125.3 3.4 %copy-start.5 = (bf16[4,2,64,512]{3,2,1,0:T(8,128)(2,1)S(1)}, bf16[4,2,64,512]{3,2,1,0:T(8,128)(2,1)}, u32[]{:S(2)}) copy-start(bf16[4,2,64,512]{3,2,1,0:T(8,128)(2,1)} %get-tuple-element.40) | copy-start | bytes 1572868
  128.7 1.7 %copy-start.2 = (bf16[4,2,64,512]{3,2,1,0:T(8,128)(2,1)S(1)}, bf16[4,2,64,512]{3,2,1,0:T(8,128)(2,1)}, u32[]{:S(2)}) copy-start(bf16[4,2,64,512]{3,2,1,0:T(8,128)(2,1)} %get-tuple-element.38) | copy-start | bytes 1572868
  130.4 1.9 %copy-start.1 = (bf16[1024,512]{1,0:T(8,128)(2,1)S(1)}, bf16[1024,512]{1,0:T(8,128)(2,1)}, u32[]{:S(2)}) copy-start(bf16[1024,512]{1,0:T(8,128)(2,1)} %get-tuple-element.29) | copy-start | bytes 3145732
  130.4 1.1 copy-start.6
  132.3 1.4 %copy-start.3 = (bf16[512,512]{1,0:T(8,128)(2,1)S(1)}, bf16[512,512]{1,0:T(8,128)(2,1)}, u32[]{:S(2)}) copy-start(bf16[512,512]{1,0:T(8,128)(2,1)} %get-tuple-element.30) | copy-start | bytes 1572868
  133.7 1.4 %copy-start = (bf16[1024,512]{1,0:T(8,128)(2,1)S(1)}, bf16[1024,512]{1,0:T(8,128)(2,1)}, u32[]{:S(2)}) copy-start(bf16[1024,512]{1,0:T(8,128)(2,1)} %get-tuple-element.31) | copy-start | bytes 3145732

commit v2 on v1

--- a/solution.py
+++ b/solution.py
@@ -17,7 +17,7 @@
 ROOT = math.sqrt(2.0 / math.pi)
 CUBE = 0.044715
 NAMES = ("dna", "dnb", "upa", "upb", "o", "q", "k", "v", "pl")
-X_FIRST = ("dna", "upa")
+ORDERS = {'dna': ('lxhy', 'hlx'), 'dnb': ('yxlh', 'Zx'), 'upa': ('xylh', 'hlx'), 'upb': ('yxlh', 'hlx'), 'o': ('yhlx', 'hlx'), 'q': ('ylxh', 'xZ'), 'k': ('yxZ', 'lhx'), 'v': ('yxZ', 'lhx'), 'pl': ('lxh', 'xhl')}
 PLAN = (
     (),
     (),
@@ -28,24 +28,25 @@
     (),
     (),
     (),
-    (),
     ("qkv.step1", "gpool.step2", "wo.step1"),
-    ("up.step1", "qkv.rx", "qkv.rz", "dn.step1", "wo.rx", "qkv.rxz"),
-    ("wo.rz",),
-    ("wo.rxz",),
-    (),
-    ("up.rx",),
-    (),
-    ("up.rz",),
-    (),
-    (),
-    (),
-    (),
-    ("dn.rx", "up.rxz"),
+    (),
+    ("up.step1", "qkv.rx", "qkv.rz", "dn.step1", "wo.rx", "wo.rz", "qkv.rxz"),
+    ("fore0.in", "wo.rxz"),
+    (),
+    (),
+    ("up.rx", "up.rz"),
+    (),
+    (),
+    ("fore1.in",),
+    (),
+    (),
+    ("up.rxz",),
+    (),
+    (),
+    (),
+    ("dn.rx", "dn.rz"),
     ("gpool.step3",),
     (),
-    ("dn.rz",),
-    (),
     (),
     ("dn.rxz",),
     (),
@@ -57,41 +58,49 @@
     (),
     (),
     (),
+    (),
+    (),
+    (),
+    (),
+    ("dnb.r0", "dna.r0"),
+    (),
+    (),
+    (),
+    (),
+    (),
     ("pooled.step2",),
-    (),
-    (),
-    ("dnb.y",),
-    ("dna.x",),
-    (),
-    ("pooled.step3",),
-    (),
-    (),
-    ("pl.x",),
-    ("dna.y",),
-    ("dnb.x",),
-    (),
-    ("upb.y",),
-    ("upa.x",),
-    (),
-    (),
-    ("dna.z", "o.y"),
-    (),
-    ("pl.z",),
-    (),
-    (),
-    (),
-    ("dnb.z", "upb.x"),
-    ("dna.gz", "v.y", "o.x"),
-    ("k.y",),
-    ("upa.y",),
-    ("q.y", "pl.gz"),
-    ("upb.z", "v.x"),
-    ("dnb.gz", "o.z"),
-    ("dna.gx", "upa.z", "v.z", "k.x", "sm.s0", "pl.gx"),
-    (),
-    ("upb.gz", "q.x"),
-    ("dnb.gx", "sm.s1", "k.z"),
-    ("dna.end", "o.gz", "late.tp", "upa.gz", "v.gz", "pl.end", "q.z", "upb.gx", "k.gz", "dnb.end", "sm.s2", "o.gx", "late.rows", "upb.end", "upa.gx", "o.end", "v.gx", "q.gz", "k.gx", "upa.end", "v.end", "sm.s3", "k.end", "q.gx", "q.end"),
+    ("dnb.r1", "dna.r1"),
+    (),
+    (),
+    ("pooled.step3", "dnb.r2"),
+    (),
+    ("upb.r0",),
+    ("upa.r0", "dna.r2"),
+    ("dnb.r3",),
+    (),
+    ("pl.r0", "o.r0"),
+    (),
+    (),
+    (),
+    (),
+    ("dna.r3",),
+    (),
+    ("upb.r1", "dnb.sum", "upa.r1"),
+    (),
+    ("o.r1",),
+    ("pl.r1", "v.r0", "dna.sum"),
+    ("upb.r2", "upa.r2", "dnb.g1", "k.r0"),
+    ("q.r0",),
+    ("o.r2",),
+    ("pl.r2", "upb.r3", "v.r1", "dna.g1"),
+    ("upa.r3", "o.r3"),
+    ("dnb.end", "k.r1", "sm.s0", "v.r2", "o.sum", "q.r1", "pl.sum", "dna.g2", "k.r2", "upb.sum", "back0.in"),
+    ("upa.sum",),
+    ("pl.g1", "q.r2"),
+    ("v.sum", "o.g1", "back1.in"),
+    (),
+    ("sm.s1", "k.sum"),
+    ("dna.end", "q.r3", "upb.g1", "upa.g1", "late.tp", "v.g1", "sm.s2", "o.g2", "k.g1", "upb.g2", "upa.g2", "o.end", "pl.g2", "q.sum", "late.rows", "upb.end", "v.g2", "upa.end", "q.g1", "sm.s3", "v.end", "k.g2", "pl.end", "k.end", "q.end"),
 )
 
 
@@ -140,7 +149,7 @@
     tail = list(tail)
     sets = {}
     for name in NAMES:
-        sets[name] = [tail.pop(0) for _ in range(4 if name == "pl" else 6)]
+        sets[name] = [tail.pop(0) for _ in range(len(ORDERS[name][0]) + (2 if name == "pl" else 3))]
     if groups > 1:
         r5 = {name: tail.pop(0) for name in NAMES + ("sm", "late")}
     send_sems, recv_sems, local_sems = tail
@@ -163,6 +172,9 @@
     quad = r % 4
     rz = r + 2 - 4 * (quad // 2)
     rxz = rz + 1 - 2 * xpos
+    zh, zl = zpos // 2, zpos % 2
+    z1 = base + (zpos + 1 - 2 * zl) * 2 + xpos
+    z2 = base + ((zpos + 2) % 4) * 2 + xpos
     xzpeers = [base + ((zpos + dz) % 4) * 2 + 1 - xpos for dz in (1, 2, 3)]
     gpeers = [((r // 8 + dg) % groups) * 8 + r % 8 for dg in range(1, groups)]
 
@@ -326,6 +338,10 @@
             pl.when(t > 0)(self.right[i].wait_recv)
             pl.when(t < 3)(self.left[i].wait_recv)
 
+        def arrivals(self, name):
+            for i in range(2):
+                chain(name + str(i), ("in", functools.partial(self.wait, i), [self.left[i], self.right[i]]))
+
         def sent(self):
             for i in range(2):
                 pl.when(t > 0)(self.left[i].wait_send)
@@ -337,6 +353,8 @@
         return nw.at[pl.ds(i * HR, HR), pl.ds(first, HALO)]
 
     halo = Halo([(edges(i, HALO), edges(i, HALO + LS), edges(i, LS), edges(i, 0)) for i in range(2)])
+
+    halo.arrivals("fore")
 
     def ln1(b):
         xs = x[pl.ds(b * BT, BT), :].astype(F32)
@@ -344,7 +362,7 @@
         out = (unit * row(1) + row(2)).astype(BF)
         nw[pl.ds(b * BR, BR), HALO:HALO + LS, :] = out.reshape(BR, LS, D)
 
-    run("ln1", NB, ln1, {NB // 2 - 1: lambda: halo.send(0), NB - 1: lambda: halo.send(1)})
+    run("ln1", NB, ln1, {NB // 2 - 1: lambda: halo.send(0), NB - 1: lambda: (halo.send(1), live("fore0", "fore1"))})
 
     @pl.when(t == 0)
     def _():
@@ -478,51 +496,17 @@
     must("qkv")
     w_qkv.ready()
     run("own_far", NB, lambda b: project_own(far, b))
-    halo.wait(0)
+    must("fore0")
     run("halo_all", HB, project_halo)
     run("attend", AB, attend)
-    halo.wait(1)
+    must("fore1")
     run("halo_all", HB, lambda b: project_halo(b + HB))
     run("attend", AB, lambda i: attend(i + AB))
-    must("wo", "up", "dn")
-    for w in (w_o, w_up, w_dn):
-        w.near()
-        w.ready()
-
-    FC = FF // 4
     ids = lax.broadcasted_iota(jnp.int32, (SEGS, LS), 0).astype(F32)
 
     def chosen(n):
         return (ids == codes[pl.ds(n, 1), 0:LS]).astype(F32).astype(BF)
 
-    def feed(b):
-        rows_ = pl.ds(b * BT, BT)
-        middle = x[rows_, :].astype(F32) + (mm(at[rows_, :], wo[...]) + row(0))
-        mid[rows_, :] = middle
-        unit, _ = normalize(middle)
-        normed = (unit * row(3) + row(4)).astype(BF)
-        nf[rows_, :] = normed
-        acc = middle + row(5)
-        for j in range(4):
-            cols = slice(j * FC, (j + 1) * FC)
-            u = mm(normed, wup[:, cols]) + bup[j:j + 1, :]
-            u2 = u * u
-            th = jnp.tanh(ROOT * u * (1.0 + CUBE * u2))
-            half_up = 0.5 * (1.0 + th)
-            a = (u * half_up).astype(BF)
-            act[rows_, cols] = a
-            dact[rows_, cols] = (half_up + u * half_up * (1.0 - th) * (ROOT + (3.0 * CUBE * ROOT) * u2)).astype(BF)
-            acc = acc + mm(a, wdn[cols, :])
-        low = acc.astype(BF)
-        hid[rows_, :] = low
-        for n in range(BR):
-            first = chosen(b * BR + n)
-            pt[pl.ds((b * BR + n) * SEGS, SEGS), :] = mm(first, low[n * LS:(n + 1) * LS, :]).astype(BF)
-
-    run("feed", NB, feed)
-    store_hid = local(hid, hid_out)
-    pooled.step1()
-    live("pooled")
     must("gpool")
     gpool.ready()
     load_hg.wait()
@@ -536,35 +520,94 @@
         smalls[5:6, :] += total(low.astype(F32))
 
     run("place", NB, place)
+
+    must("wo", "up")
+    for w in (w_o, w_up):
+        w.near()
+        w.ready()
+
+    FC = FF // 4
+    def feed_up(b):
+        rows_ = pl.ds(b * BT, BT)
+        middle = x[rows_, :].astype(F32) + (mm(at[rows_, :], wo[...]) + row(0))
+        mid[rows_, :] = middle
+        unit, _ = normalize(middle)
+        normed = (unit * row(3) + row(4)).astype(BF)
+        nf[rows_, :] = normed
+        for j in range(4):
+            cols = slice(j * FC, (j + 1) * FC)
+            u = mm(normed, wup[:, cols]) + bup[j:j + 1, :]
+            u2 = u * u
+            th = jnp.tanh(u * (ROOT + (ROOT * CUBE) * u2))
+            half_up = 0.5 + 0.5 * th
+            a = u * half_up
+            act[rows_, cols] = a.astype(BF)
+            dact[rows_, cols] = (half_up + (a - a * half_up) * (2.0 * ROOT + (6.0 * CUBE * ROOT) * u2)).astype(BF)
+
+    def feed_down(b):
+        rows_ = pl.ds(b * BT, BT)
+        low = (mid[rows_, :] + (mm(act[rows_, :], wdn[...]) + row(5))).astype(BF)
+        hid[rows_, :] = low
+        for n in range(BR):
+            first = chosen(b * BR + n)
+            pt[pl.ds((b * BR + n) * SEGS, SEGS), :] = mm(first, low[n * LS:(n + 1) * LS, :]).astype(BF)
+
+    run("feed_up", NB, feed_up)
     gb = hg
 
+    mine = {"y": ypos, "h": zh, "l": zl, "x": xpos}
+    partner = {"y": (r, ty), "h": (z2, t), "l": (z1, t), "x": (rx, t)}
+    own_part = (zh, zl, xpos)
+
     class Reduce:
-        def __init__(self, name, g, r1, r2, r3, r4, o):
-            self.name, self.g, self.r1, self.r2, self.r3, self.r4, self.o = name, g, r1, r2, r3, r4, o
-            own = g
+        def __init__(self, name, g, r1, bufs, o):
+            self.name, self.g, self.r1, self.bufs, self.o = name, g, r1, bufs, o
+            axes = "hlx" if r1 is None else "yhlx"
+            lead = () if r1 is None else (core,)
+            over, gather = ORDERS[name]
+
+            def at(fixed, flip=""):
+                return tuple(1 - mine[a] if a == flip else mine[a] if a in fixed else slice(None) for a in axes)
+
+            def peer(dz):
+                z = (zpos + dz) % 4
+                return (z // 2, z % 2, xpos)
+
+            near_copies = []
             if r1 is not None:
                 self.a1 = remote(g.at[1 - core, 1 - ypos], r1.at[1 - ypos], (r, tc))
                 self.a2 = remote(g.at[1 - core, ypos], r1.at[ypos], (r, tc))
-                own = g.at[core, ypos]
-            self.own = own
-            self.middle()
-            self.d = [remote(own.at[(zpos + dz) % 4, xpos], r4.at[dz - 1], (zpeers[dz - 1], t)) for dz in (1, 2, 3)]
+                near_copies = [self.a1] if over[0] == "y" else [self.a1, self.a2]
+            moves, fixed, regions = [], "", []
+            for i, d in enumerate(over):
+                if d == "Z":
+                    tail_at = at(fixed)[:-3] + ()
+                    moves.append([remote(g.at[lead + tail_at + peer(dz)], bufs[i].at[dz - 1], (zpeers[dz - 1], t)) for dz in (1, 2, 3)])
+                    fixed += "hl"
+                else:
+                    moves.append([remote(g.at[lead + at(fixed, d)], bufs[i], partner[d])])
+                    fixed += d
+                regions.append(at(fixed))
+            links = [("r0", functools.partial(self.first, lead, at("", over[0]), near_copies, moves[0]), near_copies)]
+            for i in range(1, len(over)):
+                wait_for = moves[i - 1] + ([self.a2] if r1 is not None and i == 1 and over[0] == "y" else [])
+                links.append(("r" + str(i), functools.partial(self.middle, lead, regions[i - 1], i, wait_for, moves[i]), wait_for))
+            gathers, got = [], ""
+            for d in gather:
+                place_at = tuple(slice(None) if a in got else mine[a] for a in "hlx")
+                if d == "Z":
+                    gathers.append([remote(o.at[place_at], o.at[place_at], (zpeers[dz - 1], t)) for dz in (1, 2, 3)])
+                    got += "hl"
+                else:
+                    gathers.append([remote(o.at[place_at], o.at[place_at], partner[d])])
+                    got += d
             if groups > 1:
-                self.m = [remote(o.at[zpos, xpos], r5[name].at[i], (gpeers[i], t)) for i in range(groups - 1)]
-            self.e = [remote(o.at[zpos, xpos], o.at[zpos, xpos], (zpeers[dz - 1], t)) for dz in (1, 2, 3)]
-            self.f = remote(o.at[:, xpos], o.at[:, xpos], (rx, t))
-            ends = [("gz", self.gather_z, self.d), ("gx", self.gather_x, self.e), ("end", self.finish, [self.f])]
-            chain(name, *self.links(), *ends)
-
-        def links(self):
-            if self.r1 is None:
-                return [("x", self.x, []), ("z", self.z, [self.c])]
-            return [("y", self.y, [self.a1]), ("x", self.x, [self.a2, self.b]), ("z", self.z, [self.c])]
-
-        def middle(self):
-            if self.r1 is not None:
-                self.b = remote(self.g.at[core, 1 - ypos], self.r2, (r, ty))
-            self.c = remote(self.own.at[:, 1 - xpos], self.r3, (rx, t))
+                self.m = [remote(o.at[own_part], r5[name].at[i], (gpeers[i], t)) for i in range(groups - 1)]
+            links.append(("sum", functools.partial(self.last, lead, regions[-1], over[-1] == "Z", moves[-1], gathers[0]), moves[-1]))
+            for i in range(1, len(gather)):
+                links.append(("g" + str(i), functools.partial(self.gather, gathers[i - 1], gathers[i]), gathers[i - 1]))
+            links.append(("end", functools.partial(self.finish, gathers[-1]), gathers[-1]))
+            chain(name, *links)
 
         def core1(self):
             go(self.a1)
@@ -572,91 +615,56 @@
         def core2(self):
             go(self.a2)
 
-        def y(self):
-            self.a1.wait_recv()
-            self.g[core, 1 - ypos] = (self.g[core, 1 - ypos].astype(F32) + self.r1[1 - ypos].astype(F32)).astype(BF)
-            go(self.b)
-
-        def part(self, i):
-            acc = self.own[:, i].astype(F32)
+        def first(self, lead, region, awaited, moves):
+            for c in awaited:
+                c.wait_recv()
             if self.r1 is not None:
-                acc = acc + self.r1[ypos, :, i].astype(F32) + self.r2[:, i].astype(F32)
-            return acc
-
-        def x(self):
-            if self.r1 is not None:
-                self.a2.wait_recv()
-                self.b.wait_recv()
-                self.own[:, 1 - xpos] = self.part(1 - xpos).astype(BF)
-            go(self.c)
-
-        def z(self):
-            self.c.wait_recv()
-            self.own[:, xpos] = (self.part(xpos) + self.r3[...].astype(F32)).astype(BF)
-            for c in self.d:
+                self.g[lead + region] = (self.g[lead + region].astype(F32) + self.r1[region].astype(F32)).astype(BF)
+            go(moves[0])
+
+        def middle(self, lead, region, i, awaited, moves):
+            for c in awaited:
+                c.wait_recv()
+            acc = self.g[lead + region].astype(F32) + self.bufs[i - 1][...].astype(F32)
+            if self.r1 is not None and i == 1:
+                acc = acc + self.r1[region].astype(F32)
+            self.g[lead + region] = acc.astype(BF)
+            for c in moves:
                 go(c)
 
-        def gather_z(self):
-            for c in self.d:
+        def last(self, lead, region, direct, awaited, moves):
+            acc = self.g[lead + region].astype(F32)
+            for i, c in enumerate(awaited):
                 c.wait_recv()
-            acc = self.own[zpos, xpos].astype(F32)
-            for i in range(3):
-                acc = acc + self.r4[i].astype(F32)
-            self.o[zpos, xpos] = acc.astype(BF)
+                acc = acc + (self.bufs[-1][i] if direct else self.bufs[-1][...]).astype(F32)
+            self.o[own_part] = acc.astype(BF)
             if groups > 1:
                 for c in self.m:
                     c.start()
                 for c in self.m:
                     c.wait()
-                acc = self.o[zpos, xpos].astype(F32)
+                acc = self.o[own_part].astype(F32)
                 for i in range(groups - 1):
                     acc = acc + r5[self.name][i].astype(F32)
-                self.o[zpos, xpos] = acc.astype(BF)
-            for c in self.e:
+                self.o[own_part] = acc.astype(BF)
+            for c in moves:
                 go(c)
 
-        def gather_x(self):
-            for c in self.e:
+        def gather(self, awaited, moves):
+            for c in awaited:
                 c.wait_recv()
-            go(self.f)
-
-        def finish(self):
-            self.f.wait_recv()
+            for c in moves:
+                go(c)
+
+        def finish(self, awaited):
+            for c in awaited:
+                c.wait_recv()
             stores.append(local(self.o, final[self.name]))
 
-    class ReduceX(Reduce):
-        def links(self):
-            return [("x", self.x, [self.a1, self.a2]), ("y", self.y, [self.c]), ("z", self.z, [self.b])]
-
-        def middle(self):
-            self.c = remote(self.g.at[core, :, :, 1 - xpos], self.r3, (rx, t))
-            self.b = remote(self.g.at[core, 1 - ypos, :, xpos], self.r2, (r, ty))
-
-        def x(self):
-            self.a1.wait_recv()
-            self.a2.wait_recv()
-            both = self.g[core, :, :, 1 - xpos].astype(F32) + self.r1[:, :, 1 - xpos].astype(F32)
-            self.g[core, :, :, 1 - xpos] = both.astype(BF)
-            go(self.c)
-
-        def half(self, i):
-            return self.g[core, i, :, xpos].astype(F32) + self.r1[i, :, xpos].astype(F32) + self.r3[i].astype(F32)
-
-        def y(self):
-            self.c.wait_recv()
-            self.g[core, 1 - ypos, :, xpos] = self.half(1 - ypos).astype(BF)
-            go(self.b)
-
-        def z(self):
-            self.b.wait_recv()
-            self.g[core, ypos, :, xpos] = (self.half(ypos) + self.r2[...].astype(F32)).astype(BF)
-            for c in self.d:
-                go(c)
-
     HC = D // 2
 
     def halves(out, i):
-        return out.at[:, :, :, pl.ds(i * HC, HC)]
+        return out.at[:, :, :, :, pl.ds(i * HC, HC)]
 
     final = {"dna": halves(gdn_out, 0), "dnb": halves(gdn_out, 1), "upa": halves(gup_out, 0), "upb": halves(gup_out, 1),
              "o": go_out, "q": gq_out, "k": gk_out, "v": gv_out, "pl": gpl_out}
@@ -665,8 +673,8 @@
     for name in NAMES:
         held = sets[name]
         if name == "pl":
-            held = [held[0], None, None] + held[1:]
-        red[name] = (ReduceX if name in X_FIRST else Reduce)(name, *held)
+            held = [held[0], None] + held[1:]
+        red[name] = Reduce(name, held[0], held[1], held[2:-1], held[-1])
 
     def split(names, cs, ys, val):
         for i, name in enumerate(names):
@@ -686,6 +694,13 @@
 
     send1, send2 = near_cores("dna", "dnb")
     run("down_grad", 4, down_grad, {0: send1, 1: send2, 2: lambda: live("dnb"), 3: lambda: live("dna")})
+    must("dn")
+    w_dn.near()
+    w_dn.ready()
+    run("feed_down", NB, feed_down)
+    store_hid = local(hid, hid_out)
+    pooled.step1()
+    live("pooled")
 
     def feed_back(b):
         rows_ = pl.ds(b * BT, BT)
@@ -709,17 +724,6 @@
         gat[rows_, :] = mm_t(low, wo[...]).astype(BF)
 
     run("feed_back", NB, feed_back)
-    must("pooled")
-    pooled.ready()
-
-    def embed():
-        emb[...] = (mm(ps[...], wp[...]) + bp_in[...].reshape(1, D)).astype(BF)
-        sets["pl"][0][...] = t_mm(ps[...], eg[...]).astype(BF).reshape(sets["pl"][0].shape)
-        live("pl")
-
-    once("embed", embed)
-    store_emb = local(emb, emb_out)
-
     def up_grad(i):
         cs, ys = place_of(i)
         val = t_mm(nf[...], dact[:, pl.ds(pl.multiple_of((ys * 2 + cs) * FC, FC), FC)])
@@ -738,6 +742,17 @@
         live("o")
 
     once("out_grad", out_grad)
+
+    must("pooled")
+    pooled.ready()
+
+    def embed():
+        emb[...] = (mm(ps[...], wp[...]) + bp_in[...].reshape(1, D)).astype(BF)
+        sets["pl"][0][...] = t_mm(ps[...], eg[...]).astype(BF).reshape(sets["pl"][0].shape)
+        live("pl")
+
+    once("embed", embed)
+    store_emb = local(emb, emb_out)
 
     def attend_back(i):
         work = [(i * 2 + n, half) for n in range(2) for half in range(2)]
@@ -761,6 +776,7 @@
     run("attend_back", RH // 2, attend_back)
 
     back = Halo([tuple(ref.at[pl.ds(i * HR, HR)] for ref in (halo_l, halo_fr, halo_r, halo_fl)) for i in range(2)])
+    back.arrivals("back")
 
     def norm_grad(b):
         keys = pl.ds(b * BR, BR)
@@ -800,7 +816,7 @@
     once("put_v", put_value)
     once("put_k", put_key)
     once("put_q", put_query)
-    run("norm_grad", NB, norm_grad, {HB - 1: lambda: back.send(0), NB - 1: lambda: back.send(1)})
+    run("norm_grad", NB, norm_grad, {HB - 1: lambda: back.send(0), NB - 1: lambda: (back.send(1), live("back0", "back1"))})
 
     @pl.when(t == 0)
     def _():
@@ -882,9 +898,9 @@
         late[1:2, :] += total(g)
         nf[rows_, :] = (mid[rows_, :] + norm_back(g, unit, factor, row(1))).astype(BF)
 
-    back.wait(0)
+    must("back0")
     run("ln1_back", HB, ln1_back)
-    back.wait(1)
+    must("back1")
     run("ln1_back", HB, lambda b: ln1_back(b + HB))
     store_ig = local(nf, ig_out)
     for c in lates.a:
@@ -929,12 +945,13 @@
     for _ in range(2):
         scratch += [buf(RH * SEGS, D), buf(RH * SEGS // 2, D), buf(RH * SEGS // 2, D), buf(RH * SEGS, D)]
     scratch += [buf(RH * SEGS, OC), buf(16, D, dtype=F32), buf(6, 16, D, dtype=F32), buf(2, D, dtype=F32), buf(3, 2, D, dtype=F32), buf(7, 2, D, dtype=F32)]
-    for name in NAMES[:-1]:
-        c = chunk[name]
-        steps = [buf(4, *c), buf(2, 4, *c)] if name in X_FIRST else [buf(4, 2, *c), buf(4, *c)]
-        scratch += [buf(2, 2, 4, 2, *c), buf(2, 4, 2, *c)] + steps + [buf(3, *c), buf(4, 2, *c)]
-    c = chunk["pl"]
-    scratch += [buf(4, 2, *c), buf(4, *c), buf(3, *c), buf(4, 2, *c)]
+    for name in NAMES:
+        c, over = chunk[name], ORDERS[name][0]
+        left = 3 if name == "pl" else 4
+        scratch += [buf(*[2] * 3, *c)] if name == "pl" else [buf(2, *[2] * 4, *c), buf(*[2] * 4, *c)]
+        for i, d in enumerate(over):
+            scratch.append(buf(3, *c) if d == "Z" else buf(*[2] * (left - 1 - i), *c))
+        scratch.append(buf(2, 2, 2, *c))
     if groups > 1:
         scratch += [buf(groups - 1, *chunk[name]) for name in NAMES]
         scratch += [buf(groups - 1, 16, D, dtype=F32), buf(groups - 1, 2, D, dtype=F32)]
@@ -948,7 +965,7 @@
     hid, emb, ig, gdn, gup, go_, gq, gk, gv, gpl, sm, late = pl.pallas_call(
         functools.partial(layer_kernel, (groups, RH, LS, D, FF, SEGS)),
         out_shape=[out(T, D), out(RH * SEGS, OC), out(T, D)]
-        + [out(4, 2, FS // 8, D), out(4, 2, D // 8, FS)] + [out(4, 2, *chunk[name]) for name in ("o", "q", "k", "v", "pl")]
+        + [out(2, 2, 2, FS // 8, D), out(2, 2, 2, D // 8, FS)] + [out(2, 2, 2, *chunk[name]) for name in ("o", "q", "k", "v", "pl")]
         + [out(16, D, dtype=F32), out(2, D, dtype=F32)],
         in_specs=[any_, vmem, any_, vmem, any_] + [vmem] * 5 + [any_, vmem, any_, vmem, any_, vmem, any_, any_],
         out_specs=[any_] * 12,
@@ -960,22 +977,54 @@
       shift_attention, gain_feed, shift_feed, up_weight, up_bias.reshape(4, FS // 4), down_weight, down_bias,
       pool_weight, pool_bias, hidden_grad.reshape(T, D), embedding_grad.reshape(RH * SEGS, OC))
 
-    d8 = D // 4
-    return (
-        hid.reshape(RH, LS, D),
-        emb.reshape(RH, SEGS, OC),
-        ig.reshape(RH, LS, D),
-        jnp.stack([gq, gk, gv]).reshape(3, D, D // 4).astype(F32),
-        lax.dynamic_slice_in_dim(sm[6:8], t * d8, d8, 1),
-        go_.reshape(D // 4, D).astype(F32),
-        sm[0], late[0], late[1], sm[3], sm[4],
-        gup.reshape(D, FS).astype(F32),
-        lax.dynamic_slice_in_dim(sm, 8 + t, 1, 0)[0],
-        gdn.reshape(FS, D).astype(F32),
-        sm[5],
-        gpl.reshape(D, OC).astype(F32),
-        lax.dynamic_slice_in_dim(sm, 12 + t, 1, 0)[0],
-    )
+    grads = [gq, gk, gv, go_, gup, gdn, gpl]
+    flat = [(D, D // 4)] * 3 + [(D // 4, D), (D, FS), (FS, D), (D, OC)]
+    grads = [g.reshape(shape) for g, shape in zip(grads, flat)]
+    whole = [hid.reshape(RH, LS, D), emb.reshape(RH, SEGS, OC), ig.reshape(RH, LS, D)]
+    vecs = [D] * 6 + [FS, OC]
+    made = pl.pallas_call(
+        last_kernel,
+        out_shape=[out(*w.shape) for w in whole] + [out(3, D, D // 4, dtype=F32)] + [out(*shape, dtype=F32) for shape in flat[3:]]
+        + [out(2, D // 4, dtype=F32)] + [out(n, dtype=F32) for n in vecs],
+        in_specs=[any_] * 10 + [vmem] * 2,
+        out_specs=[any_] * 8 + [vmem] * 9,
+        scratch_shapes=[buf(*shape) for shape in flat] + [buf(*shape, dtype=F32) for shape in flat]
+        + [buf(*w.shape) for w in whole] + [pltpu.SemaphoreType.DMA((20,))],
+        compiler_params=pltpu.CompilerParams(vmem_limit_bytes=60 * 2 ** 20),
+        cost_estimate=pl.CostEstimate(flops=T * D, bytes_accessed=11 * 2 ** 20, transcendentals=0),
+        name="last",
+    )(*whole, *grads, sm, late)
+    hid, emb, ig, gat, go_, gup, gdn, gpl, gab, gob, ga, sa, gf, sf, gdb, gub, gpb = made
+    return (hid, emb, ig, gat, gab, go_, gob, ga, sa, gf, sf, gup, gub, gdn, gdb, gpl, gpb)
+
+
+def last_kernel(*refs):
+    whole_in, grads_in, (sm, late), refs = refs[:3], refs[3:10], refs[10:12], refs[12:]
+    whole_out, (at_out, *rest), (gab, *vec_out), refs = refs[:3], refs[3:8], refs[8:17], refs[17:]
+    low, wide, held, sems = refs[:7], refs[7:14], refs[14:17], refs[17]
+    t = lax.axis_index("tp")
+    copies = [pltpu.make_async_copy(a, b, sems.at[i]) for i, (a, b) in enumerate(zip(grads_in, low))]
+    loads = [pltpu.make_async_copy(a, b, sems.at[14 + i]) for i, (a, b) in enumerate(zip(whole_in, held))]
+    for c in loads + copies:
+        c.start()
+    n = gab.shape[1]
+    gab[...] = sm[6:8, pl.ds(pl.multiple_of(t * n, 128), n)]
+    rows = [sm[0:1, :], late[0:1, :], late[1:2, :], sm[3:4, :], sm[4:5, :], sm[5:6, :], sm[pl.ds(8 + t, 1), :], sm[pl.ds(12 + t, 1), :]]
+    for ref, value in zip(vec_out, rows):
+        ref[...] = value.reshape(ref.shape)
+    targets = [at_out.at[0], at_out.at[1], at_out.at[2]] + rest
+    stores = []
+    for i, c in enumerate(loads):
+        c.wait()
+        stores.append(pltpu.make_async_copy(held[i], whole_out[i], sems.at[17 + i]))
+        stores[-1].start()
+    for i, c in enumerate(copies):
+        c.wait()
+        wide[i][...] = low[i][...].astype(F32)
+        stores.append(pltpu.make_async_copy(wide[i], targets[i], sems.at[7 + i]))
+        stores[-1].start()
+    for c in stores:
+        c.wait()
 
 
 def solution(mesh):

time: 136 us -> 119 us (0.88)
  local copies, waits for them, and re-layouts: 6.58 us -> 0 us
  other arithmetic: 5.61 us -> 0 us
  Pallas kernels: 123 us -> 118 us
    pallas_call x1, Pallas kernels: 123 us -> 113 us  [per_device(): pl.pallas_call(functools.partial(layer_kernel, (groups, RH, LS, D, FF, SE...]
    pallas_call x0 -> x1, Pallas kernels: none -> 5.63 us  [per_device(): pl.pallas_call(last_kernel, out_shape=[out(*w.shape) for w in whole] + [o...]
    convert_element_type x4 -> x0, other arithmetic: 5.61 us -> none  [the longest x1 2.06 us: per_device(): jnp.stack([gq, gk, gv]).reshape(3, D, D // 4).astype(F32)]
    unnamed x17 -> x0, local copies, waits for them, and re-layouts: 3.8 us -> none
    dynamic_slice x2 -> x0, local copies, waits for them, and re-layouts: 2.06 us -> none  [the longest x1 1.49 us: per_device(): lax.dynamic_slice_in_dim(sm, 12 + t, 1, 0)[0]]
where the time goes in v2:
time: 119 us
  Pallas kernels  118 us (99%)
    pallas_call x1, Pallas kernels, per_device(): pl.pallas_call(functools.partial(layer_kernel, (groups, RH, LS, D, FF, SE...  113 us
    pallas_call x1, Pallas kernels, per_device(): pl.pallas_call(last_kernel, out_shape=[out(*w.shape) for w in whole] + [o...  5.63 us

profile of v2, /device:TPU:0, one launch (start us, length us, event | category | flops | bytes accessed | tf_op | source)
XLA Modules:
  0.0 119.0 jit_solution(13556256299782109424)
XLA Ops:
  0.7 112.6 %layer.1 = (bf16[1024,512]{1,0:T(8,128)(2,1)}, bf16[512,512]{1,0:T(8,128)(2,1)}, bf16[1024,512]{1,0:T(8,128)(2,1)}, bf16[2,2,2,64,512]{4,3,2,1,0:T(8,128)(2,1)},...) custom-call(bf16[1024,512]{1,0:T(8,128)(2,1)} %bitcast.24, ...), custom_call_target="tpu_custom_call" | custom-call | flops 32212254720 | bytes 20971520 | tf_op jit(solution)/shard_map/layer/pallas_call | solution.py:965
  113.2 5.6 %last.1 = (bf16[16,64,512]{2,1,0:T(8,128)(2,1)}, bf16[16,32,512]{2,1,0:T(8,128)(2,1)}, bf16[16,64,512]{2,1,0:T(8,128)(2,1)}, f32[3,512,128]{2,1,0:T(8,128)}, f32...) custom-call(bf16[16,64,512]{2,1,0:T(8,128)(2,1)} %bitcast.14, ...), custom_call_target="tpu_custom_call" | custom-call | flops 524288 | bytes 11534336 | tf_op jit(solution)/shard_map/last/pallas_call | solution.py:985

commit v3 on v2

--- a/solution.py
+++ b/solution.py
@@ -17,90 +17,72 @@
 ROOT = math.sqrt(2.0 / math.pi)
 CUBE = 0.044715
 NAMES = ("dna", "dnb", "upa", "upb", "o", "q", "k", "v", "pl")
-ORDERS = {'dna': ('lxhy', 'hlx'), 'dnb': ('yxlh', 'Zx'), 'upa': ('xylh', 'hlx'), 'upb': ('yxlh', 'hlx'), 'o': ('yhlx', 'hlx'), 'q': ('ylxh', 'xZ'), 'k': ('yxZ', 'lhx'), 'v': ('yxZ', 'lhx'), 'pl': ('lxh', 'xhl')}
+ORDERS = {'dna': ('yxZ', 'hlx'), 'dnb': ('xlyh', 'hlx'), 'upa': ('xylh', 'hlx'), 'upb': ('yxZ', 'hlx'), 'o': ('yxZ', 'lhx'), 'q': ('yxZ', 'xZ'), 'k': ('yxZ', 'lhx'), 'v': ('yxZ', 'lhx'), 'pl': ('lxh', 'xhl')}
 PLAN = (
     (),
     (),
     (),
     (),
-    (),
-    (),
-    (),
-    (),
-    (),
-    ("qkv.step1", "gpool.step2", "wo.step1"),
-    (),
-    ("up.step1", "qkv.rx", "qkv.rz", "dn.step1", "wo.rx", "wo.rz", "qkv.rxz"),
-    ("fore0.in", "wo.rxz"),
-    (),
-    (),
-    ("up.rx", "up.rz"),
-    (),
-    (),
-    ("fore1.in",),
-    (),
-    (),
-    ("up.rxz",),
-    (),
-    (),
-    (),
-    ("dn.rx", "dn.rz"),
-    ("gpool.step3",),
-    (),
-    (),
-    ("dn.rxz",),
-    (),
-    (),
-    (),
-    (),
-    (),
-    (),
-    (),
-    (),
-    (),
-    (),
-    (),
-    (),
-    (),
-    ("dnb.r0", "dna.r0"),
-    (),
-    (),
-    (),
-    (),
-    (),
-    ("pooled.step2",),
-    ("dnb.r1", "dna.r1"),
-    (),
-    (),
-    ("pooled.step3", "dnb.r2"),
-    (),
-    ("upb.r0",),
-    ("upa.r0", "dna.r2"),
-    ("dnb.r3",),
-    (),
-    ("pl.r0", "o.r0"),
-    (),
-    (),
-    (),
-    (),
-    ("dna.r3",),
-    (),
-    ("upb.r1", "dnb.sum", "upa.r1"),
-    (),
-    ("o.r1",),
-    ("pl.r1", "v.r0", "dna.sum"),
-    ("upb.r2", "upa.r2", "dnb.g1", "k.r0"),
-    ("q.r0",),
-    ("o.r2",),
-    ("pl.r2", "upb.r3", "v.r1", "dna.g1"),
-    ("upa.r3", "o.r3"),
-    ("dnb.end", "k.r1", "sm.s0", "v.r2", "o.sum", "q.r1", "pl.sum", "dna.g2", "k.r2", "upb.sum", "back0.in"),
-    ("upa.sum",),
-    ("pl.g1", "q.r2"),
-    ("v.sum", "o.g1", "back1.in"),
-    (),
-    ("sm.s1", "k.sum"),
-    ("dna.end", "q.r3", "upb.g1", "upa.g1", "late.tp", "v.g1", "sm.s2", "o.g2", "k.g1", "upb.g2", "upa.g2", "o.end", "pl.g2", "q.sum", "late.rows", "upb.end", "v.g2", "upa.end", "q.g1", "sm.s3", "v.end", "k.g2", "pl.end", "k.end", "q.end"),
+    (0, 1, 6),
+    (2,),
+    (),
+    (0, 0, 4),
+    (),
+    (),
+    (),
+    (1, 1, 5),
+    (0,),
+    (1,),
+    (),
+    (),
+    (2, 2),
+    (),
+    (),
+    (6,),
+    (),
+    (2,),
+    (3,),
+    (),
+    (),
+    (),
+    (),
+    (),
+    (3, 3),
+    (3,),
+    (),
+    (),
+    (),
+    (8,),
+    (),
+    (9,),
+    (),
+    (7,),
+    (8, 9),
+    (),
+    (),
+    (),
+    (11, 10),
+    (7, 8, 9),
+    (),
+    (12, 16),
+    (),
+    (),
+    (),
+    (),
+    (8, 11, 10),
+    (),
+    (9,),
+    (),
+    (),
+    (12, 8, 16, 11, 15, 9),
+    (10, 14),
+    (8, 12, 13),
+    (16, 11, 15, 9),
+    (10, 14, 19, 8, 12, 15, 17),
+    (16, 9, 14),
+    (12, 11, 13, 10, 16, 15, 18),
+    (11, 14, 19),
+    (9, 12, 13, 10, 20, 15, 14, 11, 19, 10, 12, 16, 13, 20, 10, 15, 13, 14, 15, 19, 16, 14, 13),
 )
 
 
@@ -141,7 +123,7 @@
     (x_in, lab_in, wqkv_in, ab_in, wo_in, v0_in, v1_in, v2_in, v3_in, v4_in, wup_in, bup_in, wdn_in, v5_in, wp_in, bp_in, hg_in, eg_in,
      hid_out, emb_out, ig_out, gdn_out, gup_out, go_out, gq_out, gk_out, gv_out, gpl_out, sm_out, late_out,
      x, hg, eg, mask, codes, wqkv, wo, wup, wdn, wp, shared, vec, bup,
-     nw, q, k, v, p, at, mid, nf, act, dact, gma, gat, hid, gnc,
+     nw, q, k, v, p, at, mid, nf, act, dact, gma, gat, hid,
      halo_l, halo_r, halo_fl, halo_fr,
      gpt, gpr1, gpr2, gps, pt, pr1, pr2, ps, emb,
      smalls, sm_r, late, late_tp, late_rows,
@@ -154,7 +136,7 @@
         r5 = {name: tail.pop(0) for name in NAMES + ("sm", "late")}
     send_sems, recv_sems, local_sems = tail
     T = RH * LS
-    BR = 4
+    BR = 8
     NB = RH // BR
     BT = BR * LS
     H2 = 4 * HEAD_DIM
@@ -196,18 +178,17 @@
         c.start()
         return c
 
-    spot, steps = [0], {}
+    spot, steps = [0], []
 
     def chain(name, *links):
-        for label, fn, _ in links:
-            steps[name + "." + label] = fn
+        steps.append([fn for fn, _ in links])
 
     def live(*names):
         pass
 
     def take(i):
-        for name in PLAN[i] if i < len(PLAN) else ():
-            steps[name]()
+        for number in PLAN[i] if i < len(PLAN) else ():
+            steps[number].pop(0)()
 
     def point():
         spot[0] += 1
@@ -281,17 +262,21 @@
     class Gather:
         def __init__(self, name):
             self.name = name
-            self.y = go(remote(own_piece(name, quad), shard(name, t, quad), (r, ty)))
-            self.c = go(remote(given[name], shard(name, t), (r, tc)))
-            self.loc = local(given[name], shard(name, t))
+            self.y = remote(own_piece(name, quad), shard(name, t, quad), (r, ty))
+            self.c = remote(given[name], shard(name, t), (r, tc))
             mine = shard(name, ty, quad)
             self.x = [remote(mine, mine, (dev, t)) for dev in (rx, rz, rxz)]
             self.f = [remote(mine, mine, (r, tc))]
             for dev in (rx, rz, rxz):
                 got = shard(name, ty, dev % 4)
                 self.f.append(remote(got, got, (r, tc)))
-            chain(name, ("step1", self.step1, [self.y]), ("rx", lambda: self.step2(0), [self.x[0]]),
-                  ("rz", lambda: self.step2(1), [self.x[1]]), ("rxz", lambda: self.step2(2), [self.x[2]]))
+            chain(name, (self.step1, [self.y]), *[(functools.partial(self.step2, i), [self.x[i]]) for i in range(3)])
+
+        def begin(self):
+            go(self.y)
+            go(self.c)
+            self.loc = local(given[self.name], shard(self.name, t))
+            live(self.name)
 
         def step1(self):
             self.y.wait_recv()
@@ -315,7 +300,8 @@
     w_o = Gather("wo")
     w_up = Gather("up")
     w_dn = Gather("dn")
-    live("qkv", "wo", "up", "dn")
+    for w in (w_qkv, w_o, w_up):
+        w.begin()
 
     for i, ref in enumerate((v0_in, v1_in, v2_in, v3_in, v4_in, v5_in)):
         vec[i:i + 1, :] = ref[...].reshape(1, D)
@@ -340,7 +326,7 @@
 
         def arrivals(self, name):
             for i in range(2):
-                chain(name + str(i), ("in", functools.partial(self.wait, i), [self.left[i], self.right[i]]))
+                chain(name + str(i), (functools.partial(self.wait, i), [self.left[i], self.right[i]]))
 
         def sent(self):
             for i in range(2):
@@ -384,7 +370,7 @@
             self.a = remote(terms.at[theirs], r1, (r, tc))
             self.b = remote(terms.at[mine], r2, (r, ty))
             self.c = remote(out.at[mine], out.at[mine], (r, tc))
-            chain(name, ("step2", self.step2, [self.a]), ("step3", self.step3, [self.b]))
+            chain(name, (self.step2, [self.a]), (self.step3, [self.b]))
 
         def step1(self):
             go(self.a)
@@ -449,15 +435,15 @@
         k[pl.ds(b * BR, BR), HALO:HALO + LS, cols] = ks.reshape(BR, LS, H2)
         v[pl.ds(b * BR, BR), HALO:HALO + LS, cols] = vs.reshape(BR, LS, H2)
 
-    def project_halo(b):
+    def project_halo(cols, b):
         rows_ = pl.ds(b * BR, BR)
         both = jnp.concatenate([nw[rows_, 0:HALO, :], nw[rows_, HALO + LS:W, :]], axis=0).reshape(BR * 2 * HALO, D)
-        ks = mm(both, wqkv[1]).astype(BF).reshape(2, BR, HALO, D)
-        vs = (mm(both, wqkv[2]) + row(7)).astype(BF).reshape(2, BR, HALO, D)
-        k[rows_, 0:HALO, :] = ks[0]
-        k[rows_, HALO + LS:W, :] = ks[1]
-        v[rows_, 0:HALO, :] = vs[0]
-        v[rows_, HALO + LS:W, :] = vs[1]
+        ks = mm(both, wqkv[1, :, cols]).astype(BF).reshape(2, BR, HALO, H2)
+        vs = (mm(both, wqkv[2, :, cols]) + vec[7:8, cols]).astype(BF).reshape(2, BR, HALO, H2)
+        k[rows_, 0:HALO, cols] = ks[0]
+        k[rows_, HALO + LS:W, cols] = ks[1]
+        v[rows_, 0:HALO, cols] = vs[0]
+        v[rows_, HALO + LS:W, cols] = vs[1]
 
     lane = lax.broadcasted_iota(jnp.int32, (1, H2), 1) // HEAD_DIM
     heads = [(lane == h).astype(F32).astype(BF) for h in range(4)]
@@ -471,37 +457,39 @@
         out = jnp.where(lane == 2, parts[2], out)
         return jnp.where(lane == 3, parts[3], out)
 
-    def attend(i):
-        work = [(i * 2 + n, half) for n in range(2) for half in range(2)]
-        sides = [slice(half * H2, (half + 1) * H2) for _, half in work]
+    def attend(half, cols, i):
+        rows4 = [i * 4 + n for n in range(4)]
         scores = []
-        for (n, _), c in zip(work, sides):
+        for n in rows4:
             m1 = mask[pl.ds(n * LS, LS), :]
-            qs = spread_heads(q[pl.ds(n * LS, LS), c])
-            scores.append(mm_t(qs, k[n, :, c]) + jnp.concatenate([m1] * 4, axis=0))
+            qs = spread_heads(q[pl.ds(n * LS, LS), cols])
+            scores.append(mm_t(qs, k[n, :, cols]) + jnp.concatenate([m1] * 4, axis=0))
         tops = [jnp.max(sc, axis=-1, keepdims=True) for sc in scores]
         es = [jnp.exp(sc - top) for sc, top in zip(scores, tops)]
         inv = [1.0 / jnp.sum(e, axis=-1, keepdims=True) for e in es]
         ws = [(e * f).astype(BF) for e, f in zip(es, inv)]
         outs = []
-        for (n, half), c, w in zip(work, sides, ws):
+        for n, w in zip(rows4, ws):
             p[pl.ds((n * 2 + half) * 4 * LS, 4 * LS), :] = w
-            outs.append(mm(w, v[n, :, c]))
-        for (n, _), c, o in zip(work, sides, outs):
-            at[pl.ds(n * LS, LS), c] = merge_heads(o).astype(BF)
+            outs.append(mm(w, v[n, :, cols]))
+        for n, o in zip(rows4, outs):
+            at[pl.ds(n * LS, LS), cols] = merge_heads(o).astype(BF)
 
     HB = NB // 2
-    AB = RH // 4
+    AB = RH // 8
     run("own_near", NB, lambda b: project_own(near, b))
+    w_dn.begin()
+    must("fore0")
+    run("halo_near", HB, lambda b: project_halo(near, b))
+    run("attend", AB, lambda i: attend(ypos, near, i))
+    must("fore1")
+    run("halo_near", HB, lambda b: project_halo(near, b + HB))
+    run("attend", AB, lambda i: attend(ypos, near, i + AB))
     must("qkv")
     w_qkv.ready()
     run("own_far", NB, lambda b: project_own(far, b))
-    must("fore0")
-    run("halo_all", HB, project_halo)
-    run("attend", AB, attend)
-    must("fore1")
-    run("halo_all", HB, lambda b: project_halo(b + HB))
-    run("attend", AB, lambda i: attend(i + AB))
+    run("halo_far", NB, lambda b: project_halo(far, b))
+    run("attend", 2 * AB, lambda i: attend(1 - ypos, far, i))
     ids = lax.broadcasted_iota(jnp.int32, (SEGS, LS), 0).astype(F32)
 
     def chosen(n):
@@ -588,10 +576,10 @@
                     moves.append([remote(g.at[lead + at(fixed, d)], bufs[i], partner[d])])
                     fixed += d
                 regions.append(at(fixed))
-            links = [("r0", functools.partial(self.first, lead, at("", over[0]), near_copies, moves[0]), near_copies)]
+            links = [(functools.partial(self.first, lead, at("", over[0]), near_copies, moves[0]), near_copies)]
             for i in range(1, len(over)):
                 wait_for = moves[i - 1] + ([self.a2] if r1 is not None and i == 1 and over[0] == "y" else [])
-                links.append(("r" + str(i), functools.partial(self.middle, lead, regions[i - 1], i, wait_for, moves[i]), wait_for))
+                links.append((functools.partial(self.middle, lead, regions[i - 1], i, wait_for, moves[i]), wait_for))
             gathers, got = [], ""
             for d in gather:
                 place_at = tuple(slice(None) if a in got else mine[a] for a in "hlx")
@@ -603,10 +591,10 @@
                     got += d
             if groups > 1:
                 self.m = [remote(o.at[own_part], r5[name].at[i], (gpeers[i], t)) for i in range(groups - 1)]
-            links.append(("sum", functools.partial(self.last, lead, regions[-1], over[-1] == "Z", moves[-1], gathers[0]), moves[-1]))
+            links.append((functools.partial(self.last, lead, regions[-1], over[-1] == "Z", moves[-1], gathers[0]), moves[-1]))
             for i in range(1, len(gather)):
-                links.append(("g" + str(i), functools.partial(self.gather, gathers[i - 1], gathers[i]), gathers[i - 1]))
-            links.append(("end", functools.partial(self.finish, gathers[-1]), gathers[-1]))
+                links.append((functools.partial(self.gather, gathers[i - 1], gathers[i]), gathers[i - 1]))
+            links.append((functools.partial(self.finish, gathers[-1]), gathers[-1]))
             chain(name, *links)
 
         def core1(self):
@@ -786,7 +774,7 @@
         smalls[7:8, :] += total(dvs.astype(F32))
         win = (mm_t(dks, wqkv[1]) + mm_t(dvs, wqkv[2])).reshape(BR, W, D)
         own = win[:, HALO:HALO + LS, :].reshape(BT, D) + mm_t(dqs, wqkv[0])
-        gnc[pl.ds(b * BT, BT), :] = own
+        gat[pl.ds(b * BT, BT), :] = own.astype(BF)
         halo_l[keys] = win[:, 0:HALO, :].astype(BF)
         halo_r[keys] = win[:, HALO + LS:W, :].astype(BF)
 
@@ -833,7 +821,7 @@
             self.copies = [[remote(smalls, sm_r.at[0], (r, tc))], [remote(smalls, sm_r.at[1], (r, ty))],
                            [remote(smalls, sm_r.at[2], (rx, t))],
                            [remote(smalls, sm_r.at[2 + dz], (zpeers[dz - 1], t)) for dz in (1, 2, 3)]]
-            chain("sm", *[("s" + str(i), functools.partial(self.step, i), self.copies[i]) for i in range(4)])
+            chain("sm", *[(functools.partial(self.step, i), self.copies[i]) for i in range(4)])
 
         def send(self, i):
             for c in self.copies[i]:
@@ -856,7 +844,7 @@
         def __init__(self):
             self.a = [remote(late, late_tp.at[i], (r, dev)) for i, dev in enumerate((tc, ty, tdiag))]
             self.b = [remote(late, late_rows.at[i], (dev, t)) for i, dev in enumerate([rx] + zpeers + xzpeers)]
-            chain("late", ("tp", self.over_tp, self.a), ("rows", self.over_rows, self.b))
+            chain("late", (self.over_tp, self.a), (self.over_rows, self.b))
 
         def over_tp(self):
             for c in self.a:
@@ -890,7 +878,7 @@
     def ln1_back(b):
         rows_ = pl.ds(b * BT, BT)
         grp = pl.ds(b * BR, BR)
-        g = gnc[rows_, :].reshape(BR, LS, D)
+        g = gat[rows_, :].astype(F32).reshape(BR, LS, D)
         g = jnp.concatenate([g[:, 0:HALO, :] + halo_fl[grp].astype(F32), g[:, HALO:LS, :] + halo_fr[grp].astype(F32)], axis=1)
         g = g.reshape(BT, D)
         unit, factor = normalize(x[rows_, :].astype(F32))
@@ -925,7 +913,7 @@
     FF = FS * 4
     W = LS + 2 * HALO
     T = RH * LS
-    NB = RH // 4
+    NB = RH // 8
     groups = rows_size // 8
     t = lax.axis_index("tp")
     part = (D // 8, D // 4)
@@ -939,7 +927,7 @@
         buf(T, D), buf(T, D), buf(RH * SEGS, OC), buf(T, W, dtype=F32), buf(RH, W, dtype=F32),
         buf(3, D, D), buf(D, D), buf(D, FF), buf(FF, D), buf(D, OC), buf(4, 8, 128, dtype=F32), buf(8, D, dtype=F32), buf(4, FS, dtype=F32),
         buf(RH, W, D), buf(T, D), buf(RH, W, D), buf(RH, W, D), buf(RH * 2 * 4 * LS, W), buf(T, D), buf(T, D, dtype=F32),
-        buf(T, D), buf(T, FF), buf(T, FF), buf(T, D), buf(T, D), buf(T, D), buf(T, D, dtype=F32),
+        buf(T, D), buf(T, FF), buf(T, FF), buf(T, D), buf(T, D), buf(T, D),
         buf(RH, HALO, D), buf(RH, HALO, D), buf(RH, HALO, D), buf(RH, HALO, D),
     ]
     for _ in range(2):

time: 119 us -> 117 us (0.983)
  Pallas kernels: 118 us -> 116 us
    pallas_call x1, Pallas kernels: 113 us -> 110 us  [per_device(): pl.pallas_call(functools.partial(layer_kernel, (groups, RH, LS, D, FF, SE...]
where the time goes in v3:
time: 117 us
  Pallas kernels  116 us (99%)
    pallas_call x1, Pallas kernels, per_device(): pl.pallas_call(functools.partial(layer_kernel, (groups, RH, LS, D, FF, SE...  110 us
    pallas_call x1, Pallas kernels, per_device(): pl.pallas_call(last_kernel, out_shape=[out(*w.shape) for w in whole] + [o...  5.63 us

profile of v3, /device:TPU:0, one launch (start us, length us, event | category | flops | bytes accessed | tf_op | source)
XLA Modules:
  0.0 116.7 jit_solution(15505255992978188576)
XLA Ops:
  0.7 110.3 %layer.1 = (bf16[1024,512]{1,0:T(8,128)(2,1)}, bf16[512,512]{1,0:T(8,128)(2,1)}, bf16[1024,512]{1,0:T(8,128)(2,1)}, bf16[2,2,2,64,512]{4,3,2,1,0:T(8,128)(2,1)},...) custom-call(bf16[1024,512]{1,0:T(8,128)(2,1)} %bitcast.24, ...), custom_call_target="tpu_custom_call" | custom-call | flops 32212254720 | bytes 20971520 | tf_op jit(solution)/shard_map/layer/pallas_call | solution.py:953
  111.0 5.6 %last.1 = (bf16[16,64,512]{2,1,0:T(8,128)(2,1)}, bf16[16,32,512]{2,1,0:T(8,128)(2,1)}, bf16[16,64,512]{2,1,0:T(8,128)(2,1)}, f32[3,512,128]{2,1,0:T(8,128)}, f32...) custom-call(bf16[16,64,512]{2,1,0:T(8,128)(2,1)} %bitcast.14, ...), custom_call_target="tpu_custom_call" | custom-call | flops 524288 | bytes 11534336 | tf_op jit(solution)/shard_map/last/pallas_call | solution.py:973

commit v4 on v3

--- a/solution.py
+++ b/solution.py
@@ -17,44 +17,54 @@
 ROOT = math.sqrt(2.0 / math.pi)
 CUBE = 0.044715
 NAMES = ("dna", "dnb", "upa", "upb", "o", "q", "k", "v", "pl")
-ORDERS = {'dna': ('yxZ', 'hlx'), 'dnb': ('xlyh', 'hlx'), 'upa': ('xylh', 'hlx'), 'upb': ('yxZ', 'hlx'), 'o': ('yxZ', 'lhx'), 'q': ('yxZ', 'xZ'), 'k': ('yxZ', 'lhx'), 'v': ('yxZ', 'lhx'), 'pl': ('lxh', 'xhl')}
+ORDERS = {
+    "dna": ("lxhy", "hlx"),
+    "dnb": ("xlhy", "hlx"),
+    "upa": ("xyZ", "hlx"),
+    "upb": ("ylxh", "hxl"),
+    "o": ("xylh", "Zx"),
+    "q": ("yxZ", "xZ"),
+    "k": ("yxZ", "xhl"),
+    "v": ("xlyh", "Zx"),
+    "pl": ("lxh", "hlx"),
+}
 PLAN = (
     (),
     (),
     (),
     (),
-    (0, 1, 6),
-    (2,),
-    (),
-    (0, 0, 4),
-    (),
-    (),
-    (),
-    (1, 1, 5),
-    (0,),
+    (6, 0),
     (1,),
     (),
+    (4,),
+    (),
+    (),
+    (0, 0),
+    (2, 1, 1, 0, 5),
+    (1,),
+    (),
+    (),
     (),
     (2, 2),
     (),
     (),
-    (6,),
-    (),
-    (2,),
+    (),
+    (6, 2),
+    (),
+    (),
     (3,),
     (),
     (),
     (),
     (),
-    (),
     (3, 3),
+    (),
     (3,),
     (),
     (),
     (),
-    (8,),
-    (),
-    (9,),
+    (),
+    (8, 9),
     (),
     (7,),
     (8, 9),
@@ -62,27 +72,28 @@
     (),
     (),
     (11, 10),
-    (7, 8, 9),
-    (),
-    (12, 16),
-    (),
-    (),
-    (),
-    (),
-    (8, 11, 10),
+    (7, 8, 17, 9),
+    (),
+    (16, 12),
+    (),
+    (),
+    (),
+    (),
+    (8,),
+    (10, 11, 17),
     (),
     (9,),
-    (),
-    (),
-    (12, 8, 16, 11, 15, 9),
-    (10, 14),
-    (8, 12, 13),
-    (16, 11, 15, 9),
-    (10, 14, 19, 8, 12, 15, 17),
-    (16, 9, 14),
-    (12, 11, 13, 10, 16, 15, 18),
-    (11, 14, 19),
-    (9, 12, 13, 10, 20, 15, 14, 11, 19, 10, 12, 16, 13, 20, 10, 15, 13, 14, 15, 19, 16, 14, 13),
+    (8, 17, 12, 16),
+    (10, 9, 15),
+    (14, 11, 8, 12),
+    (13, 16, 17),
+    (15, 14),
+    (10, 8, 11, 12, 9, 19),
+    (),
+    (),
+    (14, 16, 15, 13, 10, 11, 9, 12, 20),
+    (15, 13, 14),
+    (8, 10, 16, 9, 18, 14, 11, 12, 15, 10, 13, 16, 11, 18, 12, 13, 14, 15, 11, 16, 13, 14, 15),
 )
 
 
@@ -122,7 +133,7 @@
     W = LS + 2 * HALO
     (x_in, lab_in, wqkv_in, ab_in, wo_in, v0_in, v1_in, v2_in, v3_in, v4_in, wup_in, bup_in, wdn_in, v5_in, wp_in, bp_in, hg_in, eg_in,
      hid_out, emb_out, ig_out, gdn_out, gup_out, go_out, gq_out, gk_out, gv_out, gpl_out, sm_out, late_out,
-     x, hg, eg, mask, codes, wqkv, wo, wup, wdn, wp, shared, vec, bup,
+     lab, ab, bup_own, bp, vec_own, x, hg, eg, mask, codes, wqkv, wo, wup, wdn, wp, shared, vec, bup,
      nw, q, k, v, p, at, mid, nf, act, dact, gma, gat, hid,
      halo_l, halo_r, halo_fl, halo_fr,
      gpt, gpr1, gpr2, gps, pt, pr1, pr2, ps, emb,
@@ -171,12 +182,19 @@
 
     local_count = [0]
 
-    def local(src, dst):
+    def later(src, dst):
         i = local_count[0]
         local_count[0] += 1
-        c = pltpu.make_async_copy(src, dst, local_sems.at[i])
+        return pltpu.make_async_copy(src, dst, local_sems.at[i])
+
+    def local(src, dst):
+        c = later(src, dst)
         c.start()
         return c
+
+    def store(copy):
+        copy.start()
+        stores.append(copy)
 
     spot, steps = [0], []
 
@@ -225,7 +243,10 @@
         pending.append(copy)
         return copy
 
+    load_own = [local(ab_in, ab), local(bup_in, bup_own)]
     load_x = local(x_in, x)
+    load_vec = [local(ref, vec_own.at[i]) for i, ref in enumerate((v0_in, v1_in, v2_in, v3_in, v4_in, v5_in))]
+    load_lab = [local(lab_in, lab), local(bp_in, bp)]
     load_wp = local(wp_in, wp)
     load_eg = local(eg_in, eg)
     barrier = pltpu.get_barrier_semaphore()
@@ -234,8 +255,10 @@
         pl.semaphore_signal(barrier, inc=1, device_id=dev, device_id_type=MESH)
     pl.semaphore_wait(barrier, len(friends))
 
-    shared[t, 0:2, :] = ab_in[...]
-    shared[t, 2:6, :] = bup_in[...]
+    for c in load_own:
+        c.wait()
+    shared[t, 0:2, :] = ab[...]
+    shared[t, 2:6, :] = bup_own[...]
     bias_moves = [go(remote(shared.at[t], shared.at[t], (r, dev))) for dev in (tc, ty, tdiag)]
     full = {"qkv": wqkv, "wo": wo, "up": wup, "dn": wdn}
     given = {"qkv": wqkv_in, "wo": wo_in, "up": wup_in, "dn": wdn_in}
@@ -264,6 +287,7 @@
             self.name = name
             self.y = remote(own_piece(name, quad), shard(name, t, quad), (r, ty))
             self.c = remote(given[name], shard(name, t), (r, tc))
+            self.loc = later(given[name], shard(name, t))
             mine = shard(name, ty, quad)
             self.x = [remote(mine, mine, (dev, t)) for dev in (rx, rz, rxz)]
             self.f = [remote(mine, mine, (r, tc))]
@@ -275,7 +299,7 @@
         def begin(self):
             go(self.y)
             go(self.c)
-            self.loc = local(given[self.name], shard(self.name, t))
+            self.loc.start()
             live(self.name)
 
         def step1(self):
@@ -300,11 +324,12 @@
     w_o = Gather("wo")
     w_up = Gather("up")
     w_dn = Gather("dn")
-    for w in (w_qkv, w_o, w_up):
+    for w in (w_qkv, w_o):
         w.begin()
 
-    for i, ref in enumerate((v0_in, v1_in, v2_in, v3_in, v4_in, v5_in)):
-        vec[i:i + 1, :] = ref[...].reshape(1, D)
+    for c in load_vec + load_lab:
+        c.wait()
+    vec[0:6, :] = vec_own[...]
 
     def row(i):
         return vec[i:i + 1, :]
@@ -348,7 +373,7 @@
         out = (unit * row(1) + row(2)).astype(BF)
         nw[pl.ds(b * BR, BR), HALO:HALO + LS, :] = out.reshape(BR, LS, D)
 
-    run("ln1", NB, ln1, {NB // 2 - 1: lambda: halo.send(0), NB - 1: lambda: (halo.send(1), live("fore0", "fore1"))})
+    run("ln1", NB, ln1, {NB // 2 - 1: lambda: (halo.send(0), w_up.begin()), NB - 1: lambda: (halo.send(1), live("fore0", "fore1"))})
 
     @pl.when(t == 0)
     def _():
@@ -404,7 +429,7 @@
     live("gpool")
     point()
 
-    labels = lab_in[...]
+    labels = lab[...]
     SL = labels.shape[1]
     window = pltpu.roll(labels, (SL + HALO - t * LS) % SL, 1)[:, 0:W].astype(F32)
     own_lab = pltpu.roll(labels, (SL - t * LS) % SL, 1)[:, 0:W].astype(F32)
@@ -595,6 +620,7 @@
             for i in range(1, len(gather)):
                 links.append((functools.partial(self.gather, gathers[i - 1], gathers[i]), gathers[i - 1]))
             links.append((functools.partial(self.finish, gathers[-1]), gathers[-1]))
+            self.save = later(o, final[name])
             chain(name, *links)
 
         def core1(self):
@@ -647,7 +673,7 @@
         def finish(self, awaited):
             for c in awaited:
                 c.wait_recv()
-            stores.append(local(self.o, final[self.name]))
+            store(self.save)
 
     HC = D // 2
 
@@ -729,18 +755,79 @@
         red["o"].core2()
         live("o")
 
+    late[...] = jnp.zeros(late.shape, F32)
+
+    class Small:
+        name = "sm"
+
+        def __init__(self):
+            self.save = later(smalls, sm_out)
+            self.copies = [[remote(smalls, sm_r.at[0], (r, tc))], [remote(smalls, sm_r.at[1], (r, ty))],
+                           [remote(smalls, sm_r.at[2], (rx, t))],
+                           [remote(smalls, sm_r.at[2 + dz], (zpeers[dz - 1], t)) for dz in (1, 2, 3)]]
+            chain("sm", *[(functools.partial(self.step, i), self.copies[i]) for i in range(4)])
+
+        def send(self, i):
+            for c in self.copies[i]:
+                c.start()
+
+        def step(self, i):
+            for c in self.copies[i]:
+                c.wait()
+            if i < 3:
+                smalls[...] += sm_r[i]
+                self.send(i + 1)
+            else:
+                smalls[...] += sm_r[3] + sm_r[4] + sm_r[5]
+                across(smalls, "sm")
+                store(self.save)
+
+    class Late:
+        name = "late"
+
+        def __init__(self):
+            self.save = later(late, late_out)
+            self.a = [remote(late, late_tp.at[i], (r, dev)) for i, dev in enumerate((tc, ty, tdiag))]
+            self.b = [remote(late, late_rows.at[i], (dev, t)) for i, dev in enumerate([rx] + zpeers + xzpeers)]
+            chain("late", (self.over_tp, self.a), (self.over_rows, self.b))
+
+        def over_tp(self):
+            for c in self.a:
+                c.wait()
+            late[...] += late_tp[0] + late_tp[1] + late_tp[2]
+            for c in self.b:
+                c.start()
+
+        def over_rows(self):
+            for c in self.b:
+                c.wait()
+            for i in range(7):
+                late[...] += late_rows[i]
+            across(late, "late")
+            store(self.save)
+
+    def across(ref, name):
+        moves = [remote(ref, r5[name].at[i], (gpeers[i], t)) for i in range(groups - 1)]
+        for c in moves:
+            c.start()
+        for c in moves:
+            c.wait()
+        for i in range(groups - 1):
+            ref[...] += r5[name][i]
+
+    small, lates = Small(), Late()
+    small.send(0)
+    live("sm")
     once("out_grad", out_grad)
 
     must("pooled")
     pooled.ready()
 
     def embed():
-        emb[...] = (mm(ps[...], wp[...]) + bp_in[...].reshape(1, D)).astype(BF)
         sets["pl"][0][...] = t_mm(ps[...], eg[...]).astype(BF).reshape(sets["pl"][0].shape)
         live("pl")
 
     once("embed", embed)
-    store_emb = local(emb, emb_out)
 
     def attend_back(i):
         work = [(i * 2 + n, half) for n in range(2) for half in range(2)]
@@ -770,8 +857,8 @@
         keys = pl.ds(b * BR, BR)
         dqs = q[pl.ds(b * BT, BT), :]
         dks, dvs = k[keys].reshape(BR * W, D), v[keys].reshape(BR * W, D)
-        smalls[6:7, :] += total(dqs.astype(F32))
-        smalls[7:8, :] += total(dvs.astype(F32))
+        late[2:3, :] += total(dqs.astype(F32))
+        late[3:4, :] += total(dvs.astype(F32))
         win = (mm_t(dks, wqkv[1]) + mm_t(dvs, wqkv[2])).reshape(BR, W, D)
         own = win[:, HALO:HALO + LS, :].reshape(BT, D) + mm_t(dqs, wqkv[0])
         gat[pl.ds(b * BT, BT), :] = own.astype(BF)
@@ -814,66 +901,6 @@
     def _():
         halo_fr[...] = jnp.zeros(halo_fr.shape, BF)
 
-    class Small:
-        name = "sm"
-
-        def __init__(self):
-            self.copies = [[remote(smalls, sm_r.at[0], (r, tc))], [remote(smalls, sm_r.at[1], (r, ty))],
-                           [remote(smalls, sm_r.at[2], (rx, t))],
-                           [remote(smalls, sm_r.at[2 + dz], (zpeers[dz - 1], t)) for dz in (1, 2, 3)]]
-            chain("sm", *[(functools.partial(self.step, i), self.copies[i]) for i in range(4)])
-
-        def send(self, i):
-            for c in self.copies[i]:
-                c.start()
-
-        def step(self, i):
-            for c in self.copies[i]:
-                c.wait()
-            if i < 3:
-                smalls[...] += sm_r[i]
-                self.send(i + 1)
-            else:
-                smalls[...] += sm_r[3] + sm_r[4] + sm_r[5]
-                across(smalls, "sm")
-                stores.append(local(smalls, sm_out))
-
-    class Late:
-        name = "late"
-
-        def __init__(self):
-            self.a = [remote(late, late_tp.at[i], (r, dev)) for i, dev in enumerate((tc, ty, tdiag))]
-            self.b = [remote(late, late_rows.at[i], (dev, t)) for i, dev in enumerate([rx] + zpeers + xzpeers)]
-            chain("late", (self.over_tp, self.a), (self.over_rows, self.b))
-
-        def over_tp(self):
-            for c in self.a:
-                c.wait()
-            late[...] += late_tp[0] + late_tp[1] + late_tp[2]
-            for c in self.b:
-                c.start()
-
-        def over_rows(self):
-            for c in self.b:
-                c.wait()
-            for i in range(7):
-                late[...] += late_rows[i]
-            across(late, "late")
-            stores.append(local(late, late_out))
-
-    def across(ref, name):
-        moves = [remote(ref, r5[name].at[i], (gpeers[i], t)) for i in range(groups - 1)]
-        for c in moves:
-            c.start()
-        for c in moves:
-            c.wait()
-        for i in range(groups - 1):
-            ref[...] += r5[name][i]
-
-    small, lates = Small(), Late()
-    small.send(0)
-    live("sm")
-    late[...] = jnp.zeros(late.shape, F32)
 
     def ln1_back(b):
         rows_ = pl.ds(b * BT, BT)
@@ -888,6 +915,11 @@
 
     must("back0")
     run("ln1_back", HB, ln1_back)
+    def embed_out():
+        emb[...] = (mm(ps[...], wp[...]) + bp[...].reshape(1, D)).astype(BF)
+
+    once("embed_out", embed_out)
+    store_emb = local(emb, emb_out)
     must("back1")
     run("ln1_back", HB, lambda b: ln1_back(b + HB))
     store_ig = local(nf, ig_out)
@@ -924,6 +956,7 @@
         return pltpu.VMEM(shape, dtype)
 
     scratch = [
+        pltpu.VMEM(segment_labels.shape, jnp.int32), buf(2, D // 4, dtype=F32), buf(4, FS // 4, dtype=F32), buf(OC, dtype=F32), buf(6, D, dtype=F32),
         buf(T, D), buf(T, D), buf(RH * SEGS, OC), buf(T, W, dtype=F32), buf(RH, W, dtype=F32),
         buf(3, D, D), buf(D, D), buf(D, FF), buf(FF, D), buf(D, OC), buf(4, 8, 128, dtype=F32), buf(8, D, dtype=F32), buf(4, FS, dtype=F32),
         buf(RH, W, D), buf(T, D), buf(RH, W, D), buf(RH, W, D), buf(RH * 2 * 4 * LS, W), buf(T, D), buf(T, D, dtype=F32),
@@ -932,7 +965,7 @@
     ]
     for _ in range(2):
         scratch += [buf(RH * SEGS, D), buf(RH * SEGS // 2, D), buf(RH * SEGS // 2, D), buf(RH * SEGS, D)]
-    scratch += [buf(RH * SEGS, OC), buf(16, D, dtype=F32), buf(6, 16, D, dtype=F32), buf(2, D, dtype=F32), buf(3, 2, D, dtype=F32), buf(7, 2, D, dtype=F32)]
+    scratch += [buf(RH * SEGS, OC), buf(16, D, dtype=F32), buf(6, 16, D, dtype=F32), buf(4, D, dtype=F32), buf(3, 4, D, dtype=F32), buf(7, 4, D, dtype=F32)]
     for name in NAMES:
         c, over = chunk[name], ORDERS[name][0]
         left = 3 if name == "pl" else 4
@@ -942,9 +975,9 @@
         scratch.append(buf(2, 2, 2, *c))
     if groups > 1:
         scratch += [buf(groups - 1, *chunk[name]) for name in NAMES]
-        scratch += [buf(groups - 1, 16, D, dtype=F32), buf(groups - 1, 2, D, dtype=F32)]
+        scratch += [buf(groups - 1, 16, D, dtype=F32), buf(groups - 1, 4, D, dtype=F32)]
     n_remote = 4 * 9 + 3 + 8 + 6 + 9 * 11 + 6 + 10 + 11 * (groups - 1)
-    scratch += [pltpu.SemaphoreType.DMA((n_remote,)), pltpu.SemaphoreType.DMA((n_remote,)), pltpu.SemaphoreType.DMA((24,))]
+    scratch += [pltpu.SemaphoreType.DMA((n_remote,)), pltpu.SemaphoreType.DMA((n_remote,)), pltpu.SemaphoreType.DMA((48,))]
 
     def out(*shape, dtype=BF):
         return jax.ShapeDtypeStruct(shape, dtype)
@@ -954,8 +987,8 @@
         functools.partial(layer_kernel, (groups, RH, LS, D, FF, SEGS)),
         out_shape=[out(T, D), out(RH * SEGS, OC), out(T, D)]
         + [out(2, 2, 2, FS // 8, D), out(2, 2, 2, D // 8, FS)] + [out(2, 2, 2, *chunk[name]) for name in ("o", "q", "k", "v", "pl")]
-        + [out(16, D, dtype=F32), out(2, D, dtype=F32)],
-        in_specs=[any_, vmem, any_, vmem, any_] + [vmem] * 5 + [any_, vmem, any_, vmem, any_, vmem, any_, any_],
+        + [out(16, D, dtype=F32), out(4, D, dtype=F32)],
+        in_specs=[any_] * 18,
         out_specs=[any_] * 12,
         scratch_shapes=scratch,
         compiler_params=pltpu.CompilerParams(collective_id=0, has_side_effects=True, vmem_limit_bytes=63 * 2 ** 20),
@@ -974,10 +1007,10 @@
         last_kernel,
         out_shape=[out(*w.shape) for w in whole] + [out(3, D, D // 4, dtype=F32)] + [out(*shape, dtype=F32) for shape in flat[3:]]
         + [out(2, D // 4, dtype=F32)] + [out(n, dtype=F32) for n in vecs],
-        in_specs=[any_] * 10 + [vmem] * 2,
-        out_specs=[any_] * 8 + [vmem] * 9,
+        in_specs=[any_] * 12,
+        out_specs=[any_] * 17,
         scratch_shapes=[buf(*shape) for shape in flat] + [buf(*shape, dtype=F32) for shape in flat]
-        + [buf(*w.shape) for w in whole] + [pltpu.SemaphoreType.DMA((20,))],
+        + [buf(*w.shape) for w in whole] + [buf(16, D, dtype=F32), buf(4, D, dtype=F32), pltpu.SemaphoreType.DMA((31,))],
         compiler_params=pltpu.CompilerParams(vmem_limit_bytes=60 * 2 ** 20),
         cost_estimate=pl.CostEstimate(flops=T * D, bytes_accessed=11 * 2 ** 20, transcendentals=0),
         name="last",
@@ -987,30 +1020,36 @@
 
 
 def last_kernel(*refs):
-    whole_in, grads_in, (sm, late), refs = refs[:3], refs[3:10], refs[10:12], refs[12:]
+    whole_in, grads_in, small_in, refs = refs[:3], refs[3:10], refs[10:12], refs[12:]
     whole_out, (at_out, *rest), (gab, *vec_out), refs = refs[:3], refs[3:8], refs[8:17], refs[17:]
-    low, wide, held, sems = refs[:7], refs[7:14], refs[14:17], refs[17]
+    low, wide, held, (sm, late, sems) = refs[:7], refs[7:14], refs[14:17], refs[17:]
     t = lax.axis_index("tp")
-    copies = [pltpu.make_async_copy(a, b, sems.at[i]) for i, (a, b) in enumerate(zip(grads_in, low))]
-    loads = [pltpu.make_async_copy(a, b, sems.at[14 + i]) for i, (a, b) in enumerate(zip(whole_in, held))]
-    for c in loads + copies:
+    number = [0]
+
+    def copy(src, dst):
+        c = pltpu.make_async_copy(src, dst, sems.at[number[0]])
+        number[0] += 1
         c.start()
-    n = gab.shape[1]
-    gab[...] = sm[6:8, pl.ds(pl.multiple_of(t * n, 128), n)]
-    rows = [sm[0:1, :], late[0:1, :], late[1:2, :], sm[3:4, :], sm[4:5, :], sm[5:6, :], sm[pl.ds(8 + t, 1), :], sm[pl.ds(12 + t, 1), :]]
-    for ref, value in zip(vec_out, rows):
-        ref[...] = value.reshape(ref.shape)
+        return c
+
+    copies = [copy(a, b) for a, b in zip(grads_in, low)]
+    small = [copy(a, b) for a, b in zip(small_in, (sm, late))]
+    loads = [copy(a, b) for a, b in zip(whole_in, held)]
     targets = [at_out.at[0], at_out.at[1], at_out.at[2]] + rest
     stores = []
+    for i in (4, 5, 6, 3, 0, 1, 2):
+        copies[i].wait()
+        wide[i][...] = low[i][...].astype(F32)
+        stores.append(copy(wide[i], targets[i]))
+    for c in small:
+        c.wait()
+    n = gab.shape[1]
+    stores.append(copy(late.at[2:4, pl.ds(pl.multiple_of(t * n, 128), n)], gab))
+    rows = [sm.at[0], late.at[0], late.at[1], sm.at[3], sm.at[4], sm.at[5], sm.at[8 + t], sm.at[12 + t]]
+    stores += [copy(a, b) for a, b in zip(rows, vec_out)]
     for i, c in enumerate(loads):
         c.wait()
-        stores.append(pltpu.make_async_copy(held[i], whole_out[i], sems.at[17 + i]))
-        stores[-1].start()
-    for i, c in enumerate(copies):
-        c.wait()
-        wide[i][...] = low[i][...].astype(F32)
-        stores.append(pltpu.make_async_copy(wide[i], targets[i], sems.at[7 + i]))
-        stores[-1].start()
+        stores.append(copy(held[i], whole_out[i]))
     for c in stores:
         c.wait()
 

time: 117 us -> 113 us (0.966)
  Pallas kernels: 116 us -> 112 us
    pallas_call x1, Pallas kernels: 110 us -> 107 us  [per_device(): pl.pallas_call(functools.partial(layer_kernel, (groups, RH, LS, D, FF, SE...]
where the time goes in v4:
time: 113 us
  Pallas kernels  112 us (99%)
    pallas_call x1, Pallas kernels, per_device(): pl.pallas_call(functools.partial(layer_kernel, (groups, RH, LS, D, FF, SE...  107 us
    pallas_call x1, Pallas kernels, per_device(): pl.pallas_call(last_kernel, out_shape=[out(*w.shape) for w in whole] + [o...  4.52 us

profile of v4, /device:TPU:0, one launch (start us, length us, event | category | flops | bytes accessed | tf_op | source)
XLA Modules:
  0.0 112.8 jit_solution(16730335110189271706)
XLA Ops:
  0.7 107.5 %layer.1 = (bf16[1024,512]{1,0:T(8,128)(2,1)}, bf16[512,512]{1,0:T(8,128)(2,1)}, bf16[1024,512]{1,0:T(8,128)(2,1)}, bf16[2,2,2,64,512]{4,3,2,1,0:T(8,128)(2,1)},...) custom-call(bf16[1024,512]{1,0:T(8,128)(2,1)} %bitcast.24, ...), custom_call_target="tpu_custom_call" | custom-call | flops 32212254720 | bytes 20971520 | tf_op jit(solution)/shard_map/layer/pallas_call | solution.py:986
  108.1 4.5 %last.1 = (bf16[16,64,512]{2,1,0:T(8,128)(2,1)}, bf16[16,32,512]{2,1,0:T(8,128)(2,1)}, bf16[16,64,512]{2,1,0:T(8,128)(2,1)}, f32[3,512,128]{2,1,0:T(8,128)}, f32...) custom-call(bf16[16,64,512]{2,1,0:T(8,128)(2,1)} %bitcast.14, ...), custom_call_target="tpu_custom_call" | custom-call | flops 524288 | bytes 11534336 | tf_op jit(solution)/shard_map/last/pallas_call | solution.py:1006

commit v5 on v4

--- a/solution.py
+++ b/solution.py
@@ -1032,11 +1032,14 @@
         c.start()
         return c
 
+    loads = [copy(a, b) for a, b in zip(whole_in, held)]
     copies = [copy(a, b) for a, b in zip(grads_in, low)]
     small = [copy(a, b) for a, b in zip(small_in, (sm, late))]
-    loads = [copy(a, b) for a, b in zip(whole_in, held)]
     targets = [at_out.at[0], at_out.at[1], at_out.at[2]] + rest
     stores = []
+    for i, c in enumerate(loads):
+        c.wait()
+        stores.append(copy(held[i], whole_out[i]))
     for i in (4, 5, 6, 3, 0, 1, 2):
         copies[i].wait()
         wide[i][...] = low[i][...].astype(F32)
@@ -1047,9 +1050,6 @@
     stores.append(copy(late.at[2:4, pl.ds(pl.multiple_of(t * n, 128), n)], gab))
     rows = [sm.at[0], late.at[0], late.at[1], sm.at[3], sm.at[4], sm.at[5], sm.at[8 + t], sm.at[12 + t]]
     stores += [copy(a, b) for a, b in zip(rows, vec_out)]
-    for i, c in enumerate(loads):
-        c.wait()
-        stores.append(copy(held[i], whole_out[i]))
     for c in stores:
         c.wait()
 

time: 113 us -> 113 us (level)
  no operation moved by 1% of the time
where the time goes in v5:
time: 113 us
  Pallas kernels  112 us (99%)
    pallas_call x1, Pallas kernels, per_device(): pl.pallas_call(functools.partial(layer_kernel, (groups, RH, LS, D, FF, SE...  107 us
    pallas_call x1, Pallas kernels, per_device(): pl.pallas_call(last_kernel, out_shape=[out(*w.shape) for w in whole] + [o...  4.38 us

profile of v5, /device:TPU:0, one launch (start us, length us, event | category | flops | bytes accessed | tf_op | source)
XLA Modules:
  0.0 112.7 jit_solution(7352796604370057606)
XLA Ops:
  0.7 107.5 %layer.1 = (bf16[1024,512]{1,0:T(8,128)(2,1)}, bf16[512,512]{1,0:T(8,128)(2,1)}, bf16[1024,512]{1,0:T(8,128)(2,1)}, bf16[2,2,2,64,512]{4,3,2,1,0:T(8,128)(2,1)},...) custom-call(bf16[1024,512]{1,0:T(8,128)(2,1)} %bitcast.24, ...), custom_call_target="tpu_custom_call" | custom-call | flops 32212254720 | bytes 20971520 | tf_op jit(solution)/shard_map/layer/pallas_call | solution.py:986
  108.1 4.4 %last.1 = (bf16[16,64,512]{2,1,0:T(8,128)(2,1)}, bf16[16,32,512]{2,1,0:T(8,128)(2,1)}, bf16[16,64,512]{2,1,0:T(8,128)(2,1)}, f32[3,512,128]{2,1,0:T(8,128)}, f32...) custom-call(bf16[16,64,512]{2,1,0:T(8,128)(2,1)} %bitcast.14, ...), custom_call_target="tpu_custom_call" | custom-call | flops 524288 | bytes 11534336 | tf_op jit(solution)/shard_map/last/pallas_call | solution.py:1006
